TPU v7x, 128 devices: a whole 4x4x4 slice. The times are simulated.
128 devices in a mesh: lat: 16 (over z, y_hi, core), lon: 8 (over y_lo, x).
Axes of the slice: x: 4, y: 4 (y_hi: 2, y_lo: 2; y = y_hi * 2 + y_lo), z: 4, core: 2. Of those that a mesh axis runs over, the one named last changes fastest.
Arguments:
- tokens: bfloat16 [8, 96, 576, 192], P(None, 'lat', 'lon'), may hold values from -6 to 6
- bias_table: float32 [16, 4, 6, 3312], P('lat'), may hold values from -4 to 243
- index_table: int32 [144, 144], replicated, may hold values from 0 to 3311
- gain_attn: float32 [192], replicated, may hold values from 0.1 to 1.9
- w_qkv: bfloat16 [192, 576], replicated, may hold values from -0.4375 to 0.4375
- w_proj: bfloat16 [192, 192], replicated, may hold values from -0.4375 to 0.4375
- gain_mlp: float32 [192], replicated, may hold values from 0.1 to 1.9
- w_up: bfloat16 [192, 768], replicated, may hold values from -0.4375 to 0.4375
- w_down: bfloat16 [768, 192], replicated, may hold values from -0.21875 to 0.21875
Outputs:
- block_out: bfloat16 [8, 96, 576, 192], P(None, 'lat', 'lon')
All inputs are finite; a program needn't handle non-finite values.
Results may differ from a plain program's by a relative error of at most 0.013.
Values may be sent and summed in bfloat16 or wider, within the bound.
No kernel may reach another device: no remote copies, remote signals or barrier semaphores. Data moves between devices by JAX's collectives and lax.ppermute only.
A program may use at most 320 MiB of HBM per device.

v0:
```python
import jax
import jax.numpy as jnp
from jax import lax
from jax.sharding import PartitionSpec as P

HEADS = 6
HD = 32
WZ = 2
WLAT = 6
WLON = 12
WIN = 144


epsilon = 1e-05


def passed_along(block, axis, distance):
    devices = range(lax.axis_size(axis))
    route = [((i - distance) % len(devices), i) for i in devices]
    return lax.ppermute(block, axis, route)


def as_sent(value):

    def short(part):
        return part.astype(jnp.bfloat16) if part.dtype == jnp.float32 else part

    return jax.tree.map(short, value)


def normalize(values, gain):
    average = jnp.mean(values, axis=-1, keepdims=True)
    centered = values - average
    variance = jnp.mean(centered * centered, axis=-1, keepdims=True)
    return centered * lax.rsqrt(variance + epsilon) * gain


def make_codes(row_count, col_count, first_row, total_rows):
    orig_rows = (first_row + jnp.arange(row_count, dtype=jnp.int32)) % total_rows
    flags = (orig_rows >= total_rows - WLAT // 2).astype(jnp.int32)
    return jnp.broadcast_to(flags[:, None], (row_count, col_count))


def window_attention(slab, codes, bias_rows, index_table, gain_attn, w_qkv, w_proj):
    levels, tile_rows, tile_cols, features = slab.shape
    lat_windows = tile_rows // WLAT
    lon_windows = tile_cols // WLON
    level_groups = levels // WZ
    labels = codes.reshape(lat_windows, WLAT, lon_windows, WLON).transpose(0, 2, 1, 3)
    labels = jnp.tile(labels.reshape(lat_windows, lon_windows, WLAT * WLON), (1, 1, WZ))
    allowed = labels[:, :, :, None] == labels[:, :, None, :]
    pair_all = jnp.take(bias_rows.transpose(1, 0, 2, 3), index_table, axis=3)

    def one_group(inputs):
        group_slab, pair_bias = inputs
        normed = normalize(group_slab.astype(jnp.float32), gain_attn).astype(jnp.bfloat16)
        packed = jnp.dot(normed.reshape(-1, features), w_qkv, preferred_element_type=jnp.float32)
        packed = packed.astype(jnp.bfloat16).reshape(
            WZ, lat_windows, WLAT, lon_windows, WLON, 3, HEADS, HD
        )
        scores = jnp.einsum(
            "zriljhd,yrklnhd->rlhzijykn",
            packed[:, :, :, :, :, 0],
            packed[:, :, :, :, :, 1],
            preferred_element_type=jnp.float32,
        ) * HD ** (-0.5)
        scores = scores.reshape(lat_windows, lon_windows, HEADS, WIN, WIN)
        scores = scores + pair_bias[:, None]
        scores = jnp.where(allowed[:, :, None], scores, -1e30)
        attn_probs = jax.nn.softmax(scores, axis=-1).astype(jnp.bfloat16)
        attn_probs = attn_probs.reshape(
            lat_windows, lon_windows, HEADS, WZ, WLAT, WLON, WZ, WLAT, WLON
        )
        head_out = jnp.einsum(
            "rlhzijykn,yrklnhd->zriljhd",
            attn_probs,
            packed[:, :, :, :, :, 2],
            preferred_element_type=jnp.float32,
        )
        head_out = head_out.astype(jnp.bfloat16).reshape(-1, features)
        projected = jnp.dot(head_out, w_proj, preferred_element_type=jnp.float32)
        return projected.reshape(WZ, tile_rows, tile_cols, features)

    grouped = lax.map(
        one_group, (slab.reshape(level_groups, WZ, tile_rows, tile_cols, features), pair_all)
    )
    return grouped.reshape(levels, tile_rows, tile_cols, features)


def feed_forward(summed, gain_mlp, w_up, w_down):
    normed = normalize(summed, gain_mlp).astype(jnp.bfloat16)
    hidden = jax.nn.gelu(
        jnp.dot(normed, w_up, preferred_element_type=jnp.float32), approximate=False
    )
    hidden = hidden.astype(jnp.bfloat16)
    return (summed + jnp.dot(hidden, w_down, preferred_element_type=jnp.float32)).astype(
        jnp.bfloat16
    )


def mix_levels(source, attn, gain_mlp, w_up, w_down):
    levels, tile_rows, tile_cols, features = source.shape

    def one_level(inputs):
        level_tok, level_attn = inputs
        summed = level_tok.astype(jnp.float32).reshape(-1, features) + level_attn.reshape(
            -1, features
        )
        return feed_forward(summed, gain_mlp, w_up, w_down).reshape(tile_rows, tile_cols, features)

    return lax.map(one_level, (source, attn))


def shards(tokens, bias_table, index_table, gain_attn, w_qkv, w_proj, gain_mlp, w_up, w_down):
    half_lat = WLAT // 2
    half_lon = WLON // 2
    tile_rows = tokens.shape[1]
    tile_cols = tokens.shape[2]
    total_rows = tile_rows * lax.axis_size("lat")
    lat_place = lax.axis_index("lat")
    rim_tok = passed_along(tokens[:, :half_lat], "lat", -1)
    lat_tok = jnp.concatenate([tokens[:, half_lat:], rim_tok], axis=1)
    edge_tok = passed_along(lat_tok[:, :, :half_lon], "lon", -1)
    shifted = jnp.concatenate([lat_tok[:, :, half_lon:], edge_tok], axis=2)
    codes = make_codes(tile_rows, tile_cols, lat_place * tile_rows + half_lat, total_rows)
    attn_shifted = window_attention(
        shifted, codes, bias_table, index_table, gain_attn, w_qkv, w_proj
    )
    back_rows = passed_along(attn_shifted[:, -half_lat:].astype(jnp.bfloat16), "lat", 1).astype(
        jnp.float32
    )
    lat_back = jnp.concatenate([back_rows, attn_shifted[:, :-half_lat]], axis=1)
    back_cols = passed_along(as_sent(lat_back[:, :, -half_lon:]), "lon", 1)
    attn = jnp.concatenate([back_cols, lat_back[:, :, :-half_lon]], axis=2)
    block_out = mix_levels(tokens, attn, gain_mlp, w_up, w_down)
    return block_out


def solution(mesh):
    return jax.shard_map(
        shards,
        mesh=mesh,
        in_specs=(
            P(None, "lat", "lon", None),
            P("lat", None, None, None),
            P(),
            P(),
            P(),
            P(),
            P(),
            P(),
            P(),
        ),
        out_specs=P(None, "lat", "lon", None),
        check_vma=False,
    )
```

profile of v0, /device:TPU:0, one launch (start us, length us, event | category | flops | bytes accessed | tf_op | source)
XLA Modules:
  0.0 662.7 jit_solution(3303256377556403944)
XLA Ops:
  2.9 6.2 collective-permute-start
  9.3 4.8 copy.29
  14.1 60.8 %gather_fusion = f32[20736,4,6]{2,1,0:T(4,128)} fusion(f32[4,6,3312]{1,0,2:T(4,128)} %bitcast.123, s32[21504]{0:T(1024)S(1)} %pad_clamp_fusion), kind=kCustom, calls=%fused_computation | custom fusion | bytes 4064256 | tf_op jit(solution)/shard_map/jit(_take)/gather | solution.py:52
  74.9 40.7 %copy.38 = f32[144,144,4,6]{1,0,2,3:T(8,128)S(1)} copy(f32[144,144,4,6]{3,2,1,0:T(4,128)} %bitcast.121) | data formatting | bytes 3981312 | tf_op jit(solution)/shard_map/jit(_take)/gather | solution.py:52
  127.9 454.7 %while.22 = (s32[]{:T(128)}, f32[4,2,6,72,192]{4,3,2,1,0:T(8,128)}, bf16[4,2,6,72,192]{4,3,2,1,0:T(8,128)(2,1)}, f32[192]{0:T(256)S(1)}, bf16[192,576]{1,0:T(8,1...) while((s32[]{:T(128)}, f32[4,2,6,72,192]{4,3,2,1,0:T(8,128)}, ...), condition=%wide.region_5.6_spmd.clone, body=%wide.region_0.5_spmd.clone.sunk | while | flops 364156128 | bytes 49400980 | solution.py:84
  134.7 5.5 reshape.238
  140.2 5.3 fusion.134
  146.8 5.0 add.151
  151.7 9.8 %copy.79 = f32[6,2,6,12,2,6,12]{3,6,5,4,2,1,0:T(8,128)} copy(f32[6,2,6,12,2,6,12]{6,5,4,3,2,1,0:T(8,128)} %add.151) | data formatting | bytes 995328 | tf_op jit(solution)/shard_map/while/body/eval_jaxpr/add | solution.py:68
  161.6 4.3 broadcast_in_dim.85
  165.9 8.0 %copy.80 = pred[6,2,6,12,2,6,12]{3,6,5,4,2,1,0:T(8,128)(4,1)} copy(pred[6,2,6,12,2,6,12]{6,5,4,3,2,1,0:T(8,128)(4,1)} %broadcast_in_dim.85) | data formatting | bytes 248832 | tf_op jit(solution)/shard_map/while/body/eval_jaxpr/jit(_where)/broadcast_in_dim | solution.py:69
  173.9 22.2 %fusion.135 = (f32[6,6,2,6,12]{4,3,2,1,0:T(8,128)S(1)}, f32[6,6,2,6,12,2,6,12]{4,7,6,5,3,2,1,0:T(8,128)}) fusion(f32[6,2,6,12,2,6,12]{3,6,5,4,2,1,0:T(8,128)} %copy.79, pred[6,2,6,12,2,6,12]{3,6,5,4,2,1,0:T(8,128)(4,1)} %copy.80, bf16[2,1,6,6,12,1,6,32]{7,6,5,4,3,2,0,1:T(8,128)(2,1)} %get-tuple-element.261, ...), kind=kOutput, calls=%fused_computation.96.clone.1 | convolution fusion | flops 50756544 | bytes 4292352 | tf_op jit(solution)/shard_map/while/body/eval_jaxpr/zriljhd,yrklnhd->rlhzijykn/dot_general | solution.py:61
  196.1 20.6 %fusion.136 = f32[6,6,2,6,12]{4,3,2,1,0:T(8,128)S(1)} fusion(f32[6,6,2,6,12,2,6,12]{4,7,6,5,3,2,1,0:T(8,128)} %get-tuple-element.263, f32[6,6,2,6,12]{4,3,2,1,0:T(8,128)S(1)} %get-tuple-element.264, f32[6,2,6,12,2,6,12]{3,6,5,4,2,1,0:T(8,128)S(1)} %bitcast.118, pred[6,2,6,12,2,6,12]{3,6,5,4,2,1,0:T(8,128)(4,1)S(1)} %copy-done), kind=kLoop, calls=%fused_computation.95.clone.1 | loop fusion | flops 3727296 | bytes 3649536 | tf_op jit(solution)/shard_map/while/body/eval_jaxpr/reduce_sum | solution.py:70
  216.7 20.9 %fusion.137 = bf16[2,1,6,6,12,6,32]{6,4,2,0,5,3,1:T(8,128)(2,1)S(1)} fusion(bf16[2,1,6,6,12,1,6,32]{7,6,5,4,3,2,0,1:T(8,128)(2,1)} %get-tuple-element.260, f32[6,6,2,6,12,2,6,12]{4,7,6,5,3,2,1,0:T(8,128)} %get-tuple-element.263, f32[6,6,2,6,12]{4,3,2,1,0:T(8,128)S(1)} %fusion.136, f32[6,6,2,6,12]{4,3,2,1,0:T(8,128)S(1)} %get-tuple-element.264, ...), kind=kOutput, calls=%fused_computation.104.clone.1 | convolution fusion | flops 52420608 | bytes 4313088 | tf_op jit(solution)/shard_map/while/body/eval_jaxpr/rlhzijykn,yrklnhd->zriljhd/dot_general | solution.py:74
  248.3 5.5 reshape.238
  253.9 5.3 fusion.134
  260.4 5.0 add.151
  265.4 9.8 %copy.79 = f32[6,2,6,12,2,6,12]{3,6,5,4,2,1,0:T(8,128)} copy(f32[6,2,6,12,2,6,12]{6,5,4,3,2,1,0:T(8,128)} %add.151) | data formatting | bytes 995328 | tf_op jit(solution)/shard_map/while/body/eval_jaxpr/add | solution.py:68
  275.3 4.3 broadcast_in_dim.85
  279.6 8.0 %copy.80 = pred[6,2,6,12,2,6,12]{3,6,5,4,2,1,0:T(8,128)(4,1)} copy(pred[6,2,6,12,2,6,12]{6,5,4,3,2,1,0:T(8,128)(4,1)} %broadcast_in_dim.85) | data formatting | bytes 248832 | tf_op jit(solution)/shard_map/while/body/eval_jaxpr/jit(_where)/broadcast_in_dim | solution.py:69
  287.6 22.2 %fusion.135 = (f32[6,6,2,6,12]{4,3,2,1,0:T(8,128)S(1)}, f32[6,6,2,6,12,2,6,12]{4,7,6,5,3,2,1,0:T(8,128)}) fusion(f32[6,2,6,12,2,6,12]{3,6,5,4,2,1,0:T(8,128)} %copy.79, pred[6,2,6,12,2,6,12]{3,6,5,4,2,1,0:T(8,128)(4,1)} %copy.80, bf16[2,1,6,6,12,1,6,32]{7,6,5,4,3,2,0,1:T(8,128)(2,1)} %get-tuple-element.261, ...), kind=kOutput, calls=%fused_computation.96.clone.1 | convolution fusion | flops 50756544 | bytes 4292352 | tf_op jit(solution)/shard_map/while/body/eval_jaxpr/zriljhd,yrklnhd->rlhzijykn/dot_general | solution.py:61
  309.8 20.6 %fusion.136 = f32[6,6,2,6,12]{4,3,2,1,0:T(8,128)S(1)} fusion(f32[6,6,2,6,12,2,6,12]{4,7,6,5,3,2,1,0:T(8,128)} %get-tuple-element.263, f32[6,6,2,6,12]{4,3,2,1,0:T(8,128)S(1)} %get-tuple-element.264, f32[6,2,6,12,2,6,12]{3,6,5,4,2,1,0:T(8,128)S(1)} %bitcast.118, pred[6,2,6,12,2,6,12]{3,6,5,4,2,1,0:T(8,128)(4,1)S(1)} %copy-done), kind=kLoop, calls=%fused_computation.95.clone.1 | loop fusion | flops 3727296 | bytes 3649536 | tf_op jit(solution)/shard_map/while/body/eval_jaxpr/reduce_sum | solution.py:70
  330.4 20.9 %fusion.137 = bf16[2,1,6,6,12,6,32]{6,4,2,0,5,3,1:T(8,128)(2,1)S(1)} fusion(bf16[2,1,6,6,12,1,6,32]{7,6,5,4,3,2,0,1:T(8,128)(2,1)} %get-tuple-element.260, f32[6,6,2,6,12,2,6,12]{4,7,6,5,3,2,1,0:T(8,128)} %get-tuple-element.263, f32[6,6,2,6,12]{4,3,2,1,0:T(8,128)S(1)} %fusion.136, f32[6,6,2,6,12]{4,3,2,1,0:T(8,128)S(1)} %get-tuple-element.264, ...), kind=kOutput, calls=%fused_computation.104.clone.1 | convolution fusion | flops 52420608 | bytes 4313088 | tf_op jit(solution)/shard_map/while/body/eval_jaxpr/rlhzijykn,yrklnhd->zriljhd/dot_general | solution.py:74
  362.0 5.5 reshape.238
  367.6 5.3 fusion.134
  374.1 5.0 add.151
  379.1 9.8 %copy.79 = f32[6,2,6,12,2,6,12]{3,6,5,4,2,1,0:T(8,128)} copy(f32[6,2,6,12,2,6,12]{6,5,4,3,2,1,0:T(8,128)} %add.151) | data formatting | bytes 995328 | tf_op jit(solution)/shard_map/while/body/eval_jaxpr/add | solution.py:68
  389.0 4.3 broadcast_in_dim.85
  393.3 8.0 %copy.80 = pred[6,2,6,12,2,6,12]{3,6,5,4,2,1,0:T(8,128)(4,1)} copy(pred[6,2,6,12,2,6,12]{6,5,4,3,2,1,0:T(8,128)(4,1)} %broadcast_in_dim.85) | data formatting | bytes 248832 | tf_op jit(solution)/shard_map/while/body/eval_jaxpr/jit(_where)/broadcast_in_dim | solution.py:69
  401.3 22.2 %fusion.135 = (f32[6,6,2,6,12]{4,3,2,1,0:T(8,128)S(1)}, f32[6,6,2,6,12,2,6,12]{4,7,6,5,3,2,1,0:T(8,128)}) fusion(f32[6,2,6,12,2,6,12]{3,6,5,4,2,1,0:T(8,128)} %copy.79, pred[6,2,6,12,2,6,12]{3,6,5,4,2,1,0:T(8,128)(4,1)} %copy.80, bf16[2,1,6,6,12,1,6,32]{7,6,5,4,3,2,0,1:T(8,128)(2,1)} %get-tuple-element.261, ...), kind=kOutput, calls=%fused_computation.96.clone.1 | convolution fusion | flops 50756544 | bytes 4292352 | tf_op jit(solution)/shard_map/while/body/eval_jaxpr/zriljhd,yrklnhd->rlhzijykn/dot_general | solution.py:61
  423.5 20.6 %fusion.136 = f32[6,6,2,6,12]{4,3,2,1,0:T(8,128)S(1)} fusion(f32[6,6,2,6,12,2,6,12]{4,7,6,5,3,2,1,0:T(8,128)} %get-tuple-element.263, f32[6,6,2,6,12]{4,3,2,1,0:T(8,128)S(1)} %get-tuple-element.264, f32[6,2,6,12,2,6,12]{3,6,5,4,2,1,0:T(8,128)S(1)} %bitcast.118, pred[6,2,6,12,2,6,12]{3,6,5,4,2,1,0:T(8,128)(4,1)S(1)} %copy-done), kind=kLoop, calls=%fused_computation.95.clone.1 | loop fusion | flops 3727296 | bytes 3649536 | tf_op jit(solution)/shard_map/while/body/eval_jaxpr/reduce_sum | solution.py:70
  444.1 20.9 %fusion.137 = bf16[2,1,6,6,12,6,32]{6,4,2,0,5,3,1:T(8,128)(2,1)S(1)} fusion(bf16[2,1,6,6,12,1,6,32]{7,6,5,4,3,2,0,1:T(8,128)(2,1)} %get-tuple-element.260, f32[6,6,2,6,12,2,6,12]{4,7,6,5,3,2,1,0:T(8,128)} %get-tuple-element.263, f32[6,6,2,6,12]{4,3,2,1,0:T(8,128)S(1)} %fusion.136, f32[6,6,2,6,12]{4,3,2,1,0:T(8,128)S(1)} %get-tuple-element.264, ...), kind=kOutput, calls=%fused_computation.104.clone.1 | convolution fusion | flops 52420608 | bytes 4313088 | tf_op jit(solution)/shard_map/while/body/eval_jaxpr/rlhzijykn,yrklnhd->zriljhd/dot_general | solution.py:74
  475.7 5.5 reshape.238
  481.2 5.3 fusion.134
  487.8 5.0 add.151
  492.8 9.8 %copy.79 = f32[6,2,6,12,2,6,12]{3,6,5,4,2,1,0:T(8,128)} copy(f32[6,2,6,12,2,6,12]{6,5,4,3,2,1,0:T(8,128)} %add.151) | data formatting | bytes 995328 | tf_op jit(solution)/shard_map/while/body/eval_jaxpr/add | solution.py:68
  502.7 4.3 broadcast_in_dim.85
  507.0 8.0 %copy.80 = pred[6,2,6,12,2,6,12]{3,6,5,4,2,1,0:T(8,128)(4,1)} copy(pred[6,2,6,12,2,6,12]{6,5,4,3,2,1,0:T(8,128)(4,1)} %broadcast_in_dim.85) | data formatting | bytes 248832 | tf_op jit(solution)/shard_map/while/body/eval_jaxpr/jit(_where)/broadcast_in_dim | solution.py:69
  514.9 22.2 %fusion.135 = (f32[6,6,2,6,12]{4,3,2,1,0:T(8,128)S(1)}, f32[6,6,2,6,12,2,6,12]{4,7,6,5,3,2,1,0:T(8,128)}) fusion(f32[6,2,6,12,2,6,12]{3,6,5,4,2,1,0:T(8,128)} %copy.79, pred[6,2,6,12,2,6,12]{3,6,5,4,2,1,0:T(8,128)(4,1)} %copy.80, bf16[2,1,6,6,12,1,6,32]{7,6,5,4,3,2,0,1:T(8,128)(2,1)} %get-tuple-element.261, ...), kind=kOutput, calls=%fused_computation.96.clone.1 | convolution fusion | flops 50756544 | bytes 4292352 | tf_op jit(solution)/shard_map/while/body/eval_jaxpr/zriljhd,yrklnhd->rlhzijykn/dot_general | solution.py:61
  537.2 20.6 %fusion.136 = f32[6,6,2,6,12]{4,3,2,1,0:T(8,128)S(1)} fusion(f32[6,6,2,6,12,2,6,12]{4,7,6,5,3,2,1,0:T(8,128)} %get-tuple-element.263, f32[6,6,2,6,12]{4,3,2,1,0:T(8,128)S(1)} %get-tuple-element.264, f32[6,2,6,12,2,6,12]{3,6,5,4,2,1,0:T(8,128)S(1)} %bitcast.118, pred[6,2,6,12,2,6,12]{3,6,5,4,2,1,0:T(8,128)(4,1)S(1)} %copy-done), kind=kLoop, calls=%fused_computation.95.clone.1 | loop fusion | flops 3727296 | bytes 3649536 | tf_op jit(solution)/shard_map/while/body/eval_jaxpr/reduce_sum | solution.py:70
  557.8 20.9 %fusion.137 = bf16[2,1,6,6,12,6,32]{6,4,2,0,5,3,1:T(8,128)(2,1)S(1)} fusion(bf16[2,1,6,6,12,1,6,32]{7,6,5,4,3,2,0,1:T(8,128)(2,1)} %get-tuple-element.260, f32[6,6,2,6,12,2,6,12]{4,7,6,5,3,2,1,0:T(8,128)} %get-tuple-element.263, f32[6,6,2,6,12]{4,3,2,1,0:T(8,128)S(1)} %fusion.136, f32[6,6,2,6,12]{4,3,2,1,0:T(8,128)S(1)} %get-tuple-element.264, ...), kind=kOutput, calls=%fused_computation.104.clone.1 | convolution fusion | flops 52420608 | bytes 4313088 | tf_op jit(solution)/shard_map/while/body/eval_jaxpr/rlhzijykn,yrklnhd->zriljhd/dot_general | solution.py:74
  585.8 14.4 %collective-permute-done.2 = bf16[8,3,72,192]{3,2,1,0:T(8,128)(2,1)S(1)} collective-permute-done((bf16[8,3,72,192]{3,2,1,0:T(8,128)(2,1)S(1)}, bf16[8,3,72,192]{3,2,1,0:T(8,128)(2,1)S(1)}, u32[]{:S(2)}, u32[]{:S(2)}) %collective-permute-start.2) | collective-permute-done | bytes 663584 | tf_op jit(solution)/shard_map/ppermute | solution.py:20
  602.2 7.5 %collective-permute-done.3 = bf16[8,6,6,192]{3,2,1,0:T(8,128)(2,1)} collective-permute-done((bf16[8,6,6,192]{3,2,1,0:T(8,128)(2,1)}, bf16[8,6,6,192]{3,2,1,0:T(8,128)(2,1)}, u32[]{:S(2)}, u32[]{:S(2)}) %collective-permute-start.3) | collective-permute-done | bytes 110624 | tf_op jit(solution)/shard_map/ppermute | solution.py:20
  612.8 49.9 %while.21 = (s32[]{:T(128)}, bf16[8,6,72,192]{3,2,1,0:T(8,128)(2,1)}, bf16[8,6,72,192]{3,2,1,0:T(8,128)(2,1)}, f32[8,6,72,192]{3,2,1,0:T(8,128)}, f32[192]{0:T(2...) while((s32[]{:T(128)}, bf16[8,6,72,192]{3,2,1,0:T(8,128)(2,1)}, ...), condition=%wide.region_9.10_spmd, body=%wide.region_6.9_spmd.sunk | while | flops 277365184 | bytes 6346065 | solution.py:111
  614.8 3.4 fusion.126
  621.0 3.4 fusion.126
  627.3 3.4 fusion.126
  633.5 3.4 fusion.126
  (237 shorter events, 107.3 us)
Async XLA Ops:
  0.0 9.1 %copy-start.3 = (s32[144,144]{1,0:T(8,128)S(1)}, s32[144,144]{1,0:T(8,128)}, u32[]{:S(2)}) copy-start(s32[144,144]{1,0:T(8,128)} %param.15) | copy-start | bytes 248836
  0.0 9.3 %copy-start.4 = (f32[1,4,6,3312]{3,1,2,0:T(4,128)S(1)}, f32[1,4,6,3312]{3,1,2,0:T(4,128)}, u32[]{:S(2)}) copy-start(f32[1,4,6,3312]{3,1,2,0:T(4,128)} %param.14) | copy-start | bytes 953860
  2.9 116.2 %collective-permute-start = (bf16[8,3,72,192]{3,2,1,0:T(8,128)(2,1)}, bf16[8,3,72,192]{3,2,1,0:T(8,128)(2,1)}, u32[]{:S(2)}, u32[]{:S(2)}) collective-permute-start(bf16[8,3,72,192]{3,2,1,0:T(8,128)(2,1)} %get-tuple-element.158), channel_id=1, source_target_pairs={{8,0},{16,8},{24,16},{32,24},{40,32},{48,40},{56,48},{64,56},{72,6... | collective-permute-start | bytes 1990664 | tf_op jit(solution)/shard_map/ppermute | solution.py:20
  116.8 2.2 copy-start.1
  120.0 6.1 collective-permute-start.1
  124.6 3.3 copy-start.5
  165.9 30.2 %slice-start = ((s8[7077888]{0:T(1024)(128)(4,1)}), s8[2883584]{0:T(1024)(128)(4,1)S(1)}, s32[]{:S(2)}) async-start(s8[7077888]{0:T(1024)(128)(4,1)} %bitcast.117), calls=%async_computation | async-start | bytes 5767168 | tf_op jit(solution)/shard_map/while
  173.9 22.2 %slice-start.1 = ((s8[7077888]{0:T(1024)(128)(4,1)}), s8[4194304]{0:T(1024)(128)(4,1)S(1)}, s32[]{:S(2)}) async-start(s8[7077888]{0:T(1024)(128)(4,1)} %bitcast.117), calls=%async_computation.1 | async-start | bytes 8388608 | tf_op jit(solution)/shard_map/while
  173.9 22.2 %copy-start = (pred[6,2,6,12,2,6,12]{3,6,5,4,2,1,0:T(8,128)(4,1)S(1)}, pred[6,2,6,12,2,6,12]{3,6,5,4,2,1,0:T(8,128)(4,1)}, u32[]{:S(2)}) copy-start(pred[6,2,6,12,2,6,12]{3,6,5,4,2,1,0:T(8,128)(4,1)} %copy.80) | copy-start | bytes 373252 | tf_op jit(solution)/shard_map/while
  239.3 1.1 copy-start.2
  279.6 30.2 %slice-start = ((s8[7077888]{0:T(1024)(128)(4,1)}), s8[2883584]{0:T(1024)(128)(4,1)S(1)}, s32[]{:S(2)}) async-start(s8[7077888]{0:T(1024)(128)(4,1)} %bitcast.117), calls=%async_computation | async-start | bytes 5767168 | tf_op jit(solution)/shard_map/while
  287.6 22.2 %slice-start.1 = ((s8[7077888]{0:T(1024)(128)(4,1)}), s8[4194304]{0:T(1024)(128)(4,1)S(1)}, s32[]{:S(2)}) async-start(s8[7077888]{0:T(1024)(128)(4,1)} %bitcast.117), calls=%async_computation.1 | async-start | bytes 8388608 | tf_op jit(solution)/shard_map/while
  287.6 22.2 %copy-start = (pred[6,2,6,12,2,6,12]{3,6,5,4,2,1,0:T(8,128)(4,1)S(1)}, pred[6,2,6,12,2,6,12]{3,6,5,4,2,1,0:T(8,128)(4,1)}, u32[]{:S(2)}) copy-start(pred[6,2,6,12,2,6,12]{3,6,5,4,2,1,0:T(8,128)(4,1)} %copy.80) | copy-start | bytes 373252 | tf_op jit(solution)/shard_map/while
  352.9 1.1 copy-start.2
  393.3 30.2 %slice-start = ((s8[7077888]{0:T(1024)(128)(4,1)}), s8[2883584]{0:T(1024)(128)(4,1)S(1)}, s32[]{:S(2)}) async-start(s8[7077888]{0:T(1024)(128)(4,1)} %bitcast.117), calls=%async_computation | async-start | bytes 5767168 | tf_op jit(solution)/shard_map/while
  401.3 22.2 %slice-start.1 = ((s8[7077888]{0:T(1024)(128)(4,1)}), s8[4194304]{0:T(1024)(128)(4,1)S(1)}, s32[]{:S(2)}) async-start(s8[7077888]{0:T(1024)(128)(4,1)} %bitcast.117), calls=%async_computation.1 | async-start | bytes 8388608 | tf_op jit(solution)/shard_map/while
  401.3 22.2 %copy-start = (pred[6,2,6,12,2,6,12]{3,6,5,4,2,1,0:T(8,128)(4,1)S(1)}, pred[6,2,6,12,2,6,12]{3,6,5,4,2,1,0:T(8,128)(4,1)}, u32[]{:S(2)}) copy-start(pred[6,2,6,12,2,6,12]{3,6,5,4,2,1,0:T(8,128)(4,1)} %copy.80) | copy-start | bytes 373252 | tf_op jit(solution)/shard_map/while
  466.6 1.1 copy-start.2
  507.0 30.2 %slice-start = ((s8[7077888]{0:T(1024)(128)(4,1)}), s8[2883584]{0:T(1024)(128)(4,1)S(1)}, s32[]{:S(2)}) async-start(s8[7077888]{0:T(1024)(128)(4,1)} %bitcast.117), calls=%async_computation | async-start | bytes 5767168 | tf_op jit(solution)/shard_map/while
  514.9 22.2 %slice-start.1 = ((s8[7077888]{0:T(1024)(128)(4,1)}), s8[4194304]{0:T(1024)(128)(4,1)S(1)}, s32[]{:S(2)}) async-start(s8[7077888]{0:T(1024)(128)(4,1)} %bitcast.117), calls=%async_computation.1 | async-start | bytes 8388608 | tf_op jit(solution)/shard_map/while
  514.9 22.2 %copy-start = (pred[6,2,6,12,2,6,12]{3,6,5,4,2,1,0:T(8,128)(4,1)S(1)}, pred[6,2,6,12,2,6,12]{3,6,5,4,2,1,0:T(8,128)(4,1)}, u32[]{:S(2)}) copy-start(pred[6,2,6,12,2,6,12]{3,6,5,4,2,1,0:T(8,128)(4,1)} %copy.80) | copy-start | bytes 373252 | tf_op jit(solution)/shard_map/while
  580.3 1.1 copy-start.2
  584.1 16.2 %collective-permute-start.2 = (bf16[8,3,72,192]{3,2,1,0:T(8,128)(2,1)S(1)}, bf16[8,3,72,192]{3,2,1,0:T(8,128)(2,1)S(1)}, u32[]{:S(2)}, u32[]{:S(2)}) collective-permute-start(bf16[8,3,72,192]{3,2,1,0:T(8,128)(2,1)S(1)} %slice.68), channel_id=1, source_target_pairs={{120,0},{0,8},{8,16},{16,24},{24,32},{32,40},{40,48},{48,56},{56,6... | collective-permute-start | bytes 1990664 | tf_op jit(solution)/shard_map/ppermute | solution.py:20
  601.1 8.6 %collective-permute-start.3 = (bf16[8,6,6,192]{3,2,1,0:T(8,128)(2,1)}, bf16[8,6,6,192]{3,2,1,0:T(8,128)(2,1)}, u32[]{:S(2)}, u32[]{:S(2)}) collective-permute-start(bf16[8,6,6,192]{3,2,1,0:T(8,128)(2,1)} %fusion.98), channel_id=1, source_target_pairs={{7,0},{0,1},{1,2},{2,3},{3,4},{4,5},{5,6},{6,7},{15,8},{8,9},{9,10... | collective-permute-start | bytes 331784 | tf_op jit(solution)/shard_map/ppermute | solution.py:20
  610.6 2.2 copy-start.8
  612.8 2.0 copy-start.6
  612.8 2.0 copy-start.7
  619.1 2.0 copy-start.6
  619.1 2.0 copy-start.7
  625.3 2.0 copy-start.6
  625.3 2.0 copy-start.7
  631.5 2.0 copy-start.6
  631.5 2.0 copy-start.7
  637.8 2.0 copy-start.6
  637.8 2.0 copy-start.7
  644.0 2.0 copy-start.6
  644.0 2.0 copy-start.7
  650.3 2.0 copy-start.6
  650.3 2.0 copy-start.7
  656.5 2.0 copy-start.6
  656.5 2.0 copy-start.7
where the time goes:
time: 667 us; the launch traced here: 663 us
  local copies, waits for them, and re-layouts  294 us (44%)
  matrix products  210 us (31%)
  other arithmetic  123 us (18%)
  waiting for transfers between devices  23.4 us (4%)
  starting transfers between devices  10.3 us (2%)
    gather x2, local copies, waits for them, and re-layouts, window_attention(): pair_all = jnp.take(bias_rows.transpose(1, 0, 2, 3), index_table, axis=3)  102 us
    dot_general x4, matrix products, one_group(): jnp.einsum('zriljhd,yrklnhd->rlhzijykn', packed[:, :, :, :, :, 0], packed...  88.8 us
    dot_general x4, matrix products, one_group(): jnp.einsum('rlhzijykn,yrklnhd->zriljhd', attn_probs, packed[:, :, :, :, :...  83.7 us
    reduce_sum x4, other arithmetic, one_group(): attn_probs = jax.nn.softmax(scores, axis=-1).astype(jnp.bfloat16)  82.3 us
    add x8, local copies, waits for them, and re-layouts, one_group(): scores = scores + pair_bias[:, None]  59 us
    broadcast_in_dim x8, local copies, waits for them, and re-layouts, one_group(): scores = jnp.where(allowed[:, :, None], scores, -1e+30)  49.1 us
    dot_general x8, matrix products, feed_forward(): jnp.dot(hidden, w_down, preferred_element_type=jnp.float32)  27.2 us
    ppermute x4, waiting for transfers between devices, passed_along(): return lax.ppermute(block, axis, route)  23.4 us
  transfers between devices with their start and end apart: 4, of which 3 were waited for; matrix products, arithmetic and copies ran while one was open for 17% of the time, Pallas kernels for 0%

commit v1 on v0

v1 whole, which is shorter than its diff:
```python
import jax
import jax.numpy as jnp
import numpy as np
from jax import lax
from jax.experimental import pallas as pl
from jax.experimental.pallas import tpu as pltpu
from jax.sharding import PartitionSpec as P

HEADS = 6
HD = 32
C = 192
FFH = 768
ZW = 4
COLS = 72
UNITS = 12
WINS = 7
SLOT = 40
NEG = -1e30
LOG2E = 1.4426950408889634
EPS = 1e-05
F32 = jnp.float32
BF16 = jnp.bfloat16
GELU = (0.7978822019334538, 0.03634471964715062, -4.492210425823531e-05,
        -5.034912992251254e-05, 3.0967343436505324e-06, -6.630250880453595e-08)


def head_row(h):
    return h * SLOT + (8 if h >= 3 else 0)


def unit_place(c):
    return (c + 1) // 2, (c + 1) % 2


def gather_maps():
    perm = np.zeros((504, 432), np.float32)
    left = np.zeros((72, 48), np.float32)
    right = np.zeros((72, 48), np.float32)
    back = np.zeros((432, 480), np.float32)
    for c in range(-1, 13):
        m, half = unit_place(c)
        for r in range(6):
            for j in range(6):
                row = 72 * m + 36 * half + r * 6 + j
                if c == -1:
                    left[row, r * 8 + 2 + j] = 1
                elif c == 12:
                    right[row - 432, r * 8 + j] = 1
                else:
                    perm[row, r * COLS + 6 * c + j] = 1
                    back[r * COLS + 6 * c + j, c * SLOT + 4 * half + r * 6 + j] = 1
    return [x.astype(jnp.bfloat16) for x in (perm, left, right, back)]


def key_position(latw, key):
    halo, rest = divmod(key, 72)
    half, rest = divmod(rest, 36)
    dz, rest = divmod(rest, 18)
    di, j = divmod(rest, 6)
    upper = (latw == 0) == (halo == 0)
    return (dz * 6 + di + (3 if upper else 0)) * 12 + 6 * half + j


def index_maps():
    keys = np.zeros((2, 3, 48, 144), np.float32)
    lanes = np.zeros((2, 2, 3, 144, 128), np.float32)
    for latw in range(2):
        for key in range(144):
            keys[latw, key // 48, key % 48, key_position(latw, key)] = 1
        for half in range(2):
            for s in range(36):
                pos = key_position(latw, 36 * half + s)
                for third in range(3):
                    lanes[latw, half, third, pos, third * SLOT + 4 * half + s] = 1
    return keys.astype(jnp.bfloat16), lanes.astype(jnp.bfloat16)


def nt(a, b):
    return lax.dot_general(a, b, (((1,), (1,)), ((), ())), preferred_element_type=F32)


def tn(a, b):
    return lax.dot_general(a, b, (((0,), (0,)), ((), ())), preferred_element_type=F32)


def nn(a, b):
    return jnp.dot(a, b, preferred_element_type=F32)


POS = 3312
CH = 13


def bias_kernel(cut_ref, table_ref, index_ref, keys_ref, lanes_ref, out_ref, thi, tlo, lo_s, hi_s, g_s):
    for ch in range(CH):
        width = min(256, POS - 256 * ch)
        rows = jnp.concatenate([table_ref[0, z, :, 256 * ch : 256 * ch + width] for z in range(ZW)], axis=0)
        if width < 256:
            rows = jnp.concatenate([rows, jnp.zeros((24, 256 - width), F32)], axis=1)
        rows = rows * LOG2E
        top = rows.astype(BF16).astype(F32)
        thi[24 * ch : 24 * ch + 24] = top
        tlo[24 * ch : 24 * ch + 24] = rows - top
    index = index_ref[...]
    index_lo = (index & 255).astype(F32).astype(BF16)
    index_hi = (index >> 8).astype(F32).astype(BF16)
    for half in range(2):
        for part, dst in ((index_lo, lo_s), (index_hi, hi_s)):
            total = jnp.zeros((48, 128), F32)
            for third in range(3):
                rows = nt(keys_ref[third], part).astype(BF16)
                total = total + nn(rows, lanes_ref[half, third])
            dst[48 * half : 48 * half + 48] = total.astype(jnp.int32)
    top = thi[...].astype(BF16)
    low = tlo[...].astype(BF16)
    both = jnp.concatenate([top, low], axis=1)
    spread = lax.broadcasted_iota(jnp.int32, (256, 128), 0)

    def step(i, _):
        lo = lo_s[pl.ds(i, 1), :]
        hi = hi_s[pl.ds(i, 1), :]
        lo2 = lo_s[pl.ds(i + 48, 1), :]
        hi2 = hi_s[pl.ds(i + 48, 1), :]
        hot = jnp.concatenate(
            [(spread == lo).astype(F32).astype(BF16), (spread == lo2).astype(F32).astype(BF16)], axis=1
        )
        vals = nn(top, hot) + nn(low, hot)
        his = jnp.concatenate([hi, hi2], axis=1)
        his = jnp.broadcast_to(his, (24, 256))
        acc = vals[0:24]
        for ch in range(1, CH):
            acc = jnp.where(his == ch, vals[24 * ch : 24 * ch + 24], acc)
        g_s[i] = acc
        return 0

    lax.fori_loop(0, 48, step, 0, unroll=2)
    lane = lax.broadcasted_iota(jnp.int32, (8, 128), 1)
    cut = cut_ref[0] == 1
    sub = lax.broadcasted_iota(jnp.int32, (144, 1), 0)

    def arrange(z, _):
        for half in range(2):
            for tile in range(2):
                for k8 in range(6):
                    three = [
                        g_s[pl.ds(8 * k8, 8), z * HEADS + 3 * tile + h, 128 * half : 128 * half + 128]
                        for h in range(3)
                    ]
                    for third in range(3):
                        moved = [
                            three[h] if h == third else pltpu.roll(three[h], (SLOT * (h - third)) % 128, 1)
                            for h in range(3)
                        ]
                        got = jnp.where(lane < SLOT, moved[0], jnp.where(lane < 2 * SLOT, moved[1], moved[2]))
                        row = 48 * third + 8 * k8
                        if row >= 72:
                            got = jnp.where(cut, NEG, got)
                        out_ref[z, half, row : row + 8, 128 * tile : 128 * tile + 128] = got
        return 0

    for z in range(ZW):
        arrange(z, 0)


def make_bias(cut, table, index_table, keys, lanes):
    return pl.pallas_call(
        bias_kernel,
        out_shape=jax.ShapeDtypeStruct((ZW, 2, 144, 256), F32),
        in_specs=[pl.BlockSpec(memory_space=pltpu.SMEM)] + [pl.BlockSpec(memory_space=pltpu.VMEM)] * 4,
        out_specs=pl.BlockSpec(memory_space=pltpu.VMEM),
        scratch_shapes=[
            pltpu.VMEM((24 * CH, 256), F32),
            pltpu.VMEM((24 * CH, 256), F32),
            pltpu.VMEM((96, 128), jnp.int32),
            pltpu.VMEM((96, 128), jnp.int32),
            pltpu.VMEM((48, 24, 256), F32),
        ],
        compiler_params=pltpu.CompilerParams(vmem_limit_bytes=48 * 2**20),
    )(cut, table, index_table, keys, lanes)


def block_kernel(own_ref, prev_ref, next_ref, lo_ref, lh_ref, ro_ref, rh_ref, bias0_ref, bias1_ref,
                 ga_ref, wqkv_ref, wproj_ref, gm_ref, wup_ref, wdown_ref,
                 perm_ref, left_ref, right_ref, back_ref, out_ref,
                 xs, ns, qs, kvs, os_, rs):
    latw = pl.program_id(1)
    first = latw == 0

    def flat(v):
        return v.astype(F32).reshape(-1, C).astype(BF16)

    own = flat(own_ref[...])
    halo = flat(jnp.where(first, prev_ref[...].astype(F32), next_ref[...].astype(F32)))
    perm = perm_ref[...]
    for base, block, l_ref, r_ref in ((0, own, lo_ref, ro_ref), (72, halo, lh_ref, rh_ref)):
        got = nn(perm, block)
        edge_l = nn(left_ref[...], flat(l_ref[...]))
        edge_r = nn(right_ref[...], flat(r_ref[...]))
        for m in range(WINS):
            piece = got[72 * m : 72 * m + 72]
            if m == 0:
                piece = piece + edge_l
            if m == WINS - 1:
                piece = piece + edge_r
            xs[144 * m + base : 144 * m + base + 72] = piece
    ones = jnp.ones((C, 128), BF16)
    gain = ga_ref[...]

    def both(v):
        return jnp.concatenate([v, v[:, : C - 128]], axis=1)

    for m in range(WINS):
        x = xs[144 * m : 144 * m + 144]
        mean = both(nn(x.astype(BF16), ones) * (1.0 / C))
        cen = x - mean
        var = nn((cen * cen).astype(BF16), ones) * (1.0 / C)
        inv = both(lax.rsqrt(var + EPS))
        ns[144 * m : 144 * m + 144] = (cen * inv * gain).astype(BF16)
    packed = nn(ns[...], wqkv_ref[...])
    qs[...] = packed[:, :C] * (HD ** -0.5 * LOG2E)
    kvs[...] = packed[:, C:].astype(BF16)
    lane = lax.broadcasted_iota(jnp.int32, (SLOT, C), 1) // HD
    for c in range(UNITS):
        m, half = unit_place(c)
        q = qs[144 * m + 32 * half : 144 * m + 32 * half + SLOT]
        pad = jnp.zeros((8, C), F32)
        rows = []
        for h in range(HEADS):
            rows.append(jnp.where(lane == h, q, 0.0))
            if h in (2, 5):
                rows.append(pad)
        qm = jnp.concatenate(rows, axis=0).astype(BF16)
        k = kvs[144 * m : 144 * m + 144, :C]
        v = kvs[144 * m : 144 * m + 144, C:]
        bias = jnp.where(first, bias0_ref[0, half], bias1_ref[0, half])
        s = nt(k, qm) + bias
        e = jnp.exp2(s - jnp.max(s, axis=0, keepdims=True))
        p = (e * (1.0 / jnp.sum(e, axis=0, keepdims=True))).astype(BF16)
        o = tn(p, v)
        out = o[0:SLOT]
        for h in range(1, HEADS):
            out = jnp.where(lane == h, o[head_row(h) : head_row(h) + SLOT], out)
        os_[SLOT * c : SLOT * c + SLOT] = out
        rs[SLOT * c : SLOT * c + SLOT] = xs[144 * m + 32 * half : 144 * m + 32 * half + SLOT]
    resid = rs[...] + nn(os_[...].astype(BF16), wproj_ref[...])
    mean = jnp.mean(resid, axis=1, keepdims=True)
    cen = resid - mean
    var = nn((cen * cen).astype(BF16), ones) * (1.0 / C)
    normed = (cen * both(lax.rsqrt(var + EPS)) * gm_ref[...]).astype(BF16)
    u = nn(normed, wup_ref[...])
    w = jnp.minimum(u * u, 25.0)
    poly = jnp.full_like(w, GELU[-1])
    for coef in GELU[-2::-1]:
        poly = poly * w + coef
    hu = 0.5 * u
    hidden = (hu + hu * jnp.tanh(u * poly)).astype(BF16)
    out = (resid + nn(hidden, wdown_ref[...])).astype(BF16)
    out_ref[...] = nn(back_ref[...], out).reshape(2, 3, COLS, C).astype(BF16)


def run_block(tokens, prev, nxt, left, right, bias0, bias1, ga, wqkv, wproj, gm, wup, wdown, maps):
    perm, lmap, rmap, back = maps
    whole = lambda shape: pl.BlockSpec(shape, lambda z, w: (0,) * len(shape))
    rows3 = (2, 3, COLS, C)
    edge = (2, 3, 8, C)
    return pl.pallas_call(
        block_kernel,
        grid=(ZW, 2),
        out_shape=jax.ShapeDtypeStruct(tokens.shape, BF16),
        in_specs=[
            pl.BlockSpec(rows3, lambda z, w: (z, w, 0, 0)),
            pl.BlockSpec(rows3, lambda z, w: (z, 0, 0, 0)),
            pl.BlockSpec(rows3, lambda z, w: (z, 0, 0, 0)),
            pl.BlockSpec(edge, lambda z, w: (z, 1 + w, 0, 0)),
            pl.BlockSpec(edge, lambda z, w: (z, 3 * w, 0, 0)),
            pl.BlockSpec(edge, lambda z, w: (z, 1 + w, 0, 0)),
            pl.BlockSpec(edge, lambda z, w: (z, 3 * w, 0, 0)),
            pl.BlockSpec((1, 2, 144, 256), lambda z, w: (z, 0, 0, 0)),
            pl.BlockSpec((1, 2, 144, 256), lambda z, w: (z, 0, 0, 0)),
            whole((1, C)), whole((C, 3 * C)), whole((C, C)), whole((1, C)), whole((C, FFH)), whole((FFH, C)),
            whole((504, 432)), whole((72, 48)), whole((72, 48)), whole((432, 480)),
        ],
        out_specs=pl.BlockSpec(rows3, lambda z, w: (z, w, 0, 0)),
        scratch_shapes=[
            pltpu.VMEM((1008, C), F32),
            pltpu.VMEM((1008, C), BF16),
            pltpu.VMEM((1008, C), F32),
            pltpu.VMEM((1008, 2 * C), BF16),
            pltpu.VMEM((480, C), F32),
            pltpu.VMEM((480, C), F32),
        ],
        compiler_params=pltpu.CompilerParams(vmem_limit_bytes=56 * 2**20),
    )(tokens, prev, nxt, left, left, right, right, bias0, bias1, ga, wqkv, wproj, gm, wup, wdown,
      perm, lmap, rmap, back)


def passed_along(block, axis, distance):
    count = lax.axis_size(axis)
    return lax.ppermute(block, axis, [((i - distance) % count, i) for i in range(count)])


def shards(tokens, bias_table, index_table, gain_attn, w_qkv, w_proj, gain_mlp, w_up, w_down):
    place = lax.axis_index("lat")
    last = lax.axis_size("lat") - 1
    prev_table = passed_along(bias_table, "lat", 1)
    prev = passed_along(tokens[:, 3:], "lat", 1)
    nxt = passed_along(tokens[:, :3], "lat", -1)
    rim_l = jnp.concatenate([prev[:, :, :8], tokens[:, :, :8], nxt[:, :, :8]], axis=1)
    rim_r = jnp.concatenate([prev[:, :, -8:], tokens[:, :, -8:], nxt[:, :, -8:]], axis=1)
    right = passed_along(rim_l, "lon", -1)
    left = passed_along(rim_r, "lon", 1)
    keys, lanes = index_maps()
    maps = gather_maps()
    cut1 = (place == last).astype(jnp.int32).reshape(1)
    cut0 = (place == 0).astype(jnp.int32).reshape(1)
    bias1 = make_bias(cut1, bias_table, index_table, keys[1], lanes[1])
    bias0 = make_bias(cut0, prev_table, index_table, keys[0], lanes[0])
    return run_block(tokens, prev, nxt, left, right, bias0, bias1,
                     gain_attn.reshape(1, C), w_qkv, w_proj, gain_mlp.reshape(1, C), w_up, w_down, maps)


def solution(mesh):
    return jax.shard_map(
        shards,
        mesh=mesh,
        in_specs=(
            P(None, "lat", "lon", None),
            P("lat", None, None, None),
            P(),
            P(),
            P(),
            P(),
            P(),
            P(),
            P(),
        ),
        out_specs=P(None, "lat", "lon", None),
        check_vma=False,
    )
```

time: 667 us -> 110 us (0.16)
  the two profiles are of different devices: /device:TPU:0 before, /device:TPU:8 now
where the time goes in v1:
time: 110 us
  Pallas kernels  69 us (63%)
  waiting for transfers between devices  22.8 us (21%)
  starting transfers between devices  9.39 us (9%)
  local copies, waits for them, and re-layouts  6.93 us (6%)
  other arithmetic  1.83 us (2%)
    pallas_call x1, Pallas kernels, run_block(): pl.pallas_call(block_kernel, grid=(ZW, 2), out_shape=jax.ShapeDtypeStruct...  48.3 us
    ppermute x5, waiting for transfers between devices, passed_along(): lax.ppermute(block, axis, [((i - distance) % count, i) for i in range(cou...  22.8 us
    pallas_call x2, Pallas kernels, make_bias(): pl.pallas_call(bias_kernel, out_shape=jax.ShapeDtypeStruct((ZW, 2, 144, 2...  20.7 us
    ppermute x5, starting transfers between devices, passed_along(): lax.ppermute(block, axis, [((i - distance) % count, i) for i in range(cou...  9.39 us
    unnamed x28, local copies, waits for them, and re-layouts  4.13 us
  transfers between devices with their start and end apart: 5, of which 1 were waited for; matrix products, arithmetic and copies ran while one was open for 4% of the time, Pallas kernels for 19%

profile of v1, /device:TPU:8, one launch (start us, length us, event | category | flops | bytes accessed | tf_op | source)
XLA Modules:
  0.0 110.1 jit_solution(1454424335576461009)
XLA Ops:
  0.0 0.0 copy-start.11
  0.0 1.6 %fusion.1 = (bf16[8,3,72,192]{3,2,1,0:T(8,128)(2,1)S(1)}, bf16[8,3,72,192]{3,2,1,0:T(8,128)(2,1)S(1)}) fusion(bf16[8,6,72,192]{3,2,1,0:T(8,128)(2,1)} %own_ref.1), kind=kLoop, calls=%fused_computation.3 | loop fusion | bytes 2654208 | tf_op jit(solution)/shard_map/slice | solution.py:307
  1.6 5.3 %collective-permute-start.1 = (bf16[8,3,72,192]{3,2,1,0:T(8,128)(2,1)S(1)}, bf16[8,3,72,192]{3,2,1,0:T(8,128)(2,1)S(1)}, u32[]{:S(2)}, u32[]{:S(2)}) collective-permute-start(bf16[8,3,72,192]{3,2,1,0:T(8,128)(2,1)S(1)} %get-tuple-element.7), channel_id=1, source_target_pairs={{8,0},{16,8},{24,16},{32,24},{40,32},{48,40},{56,48},{64,56},{72,6... | collective-permute-start | bytes 1990664 | tf_op jit(solution)/shard_map/ppermute | solution.py:299
  6.9 0.0 collective-permute-start
  6.9 0.0 copy-done.11
  6.9 0.1 copy.18.table_ref
  7.0 0.0 copy-start.12
  7.0 0.0 copy-start.2
  7.0 0.0 copy-start.4
  7.0 0.0 copy-start.6
  7.0 0.1 collective-permute-start.4
  7.1 1.2 %fusion = (bf16[8,6,8,192]{3,2,1,0:T(8,128)(2,1)S(1)}, bf16[8,6,8,192]{3,2,1,0:T(8,128)(2,1)S(1)}) fusion(bf16[8,6,72,192]{3,2,1,0:T(8,128)(2,1)} %own_ref.1), kind=kLoop, calls=%fused_computation.2 | loop fusion | bytes 589824 | tf_op jit(solution)/shard_map/slice | solution.py:308
  8.3 22.8 %collective-permute-done.1.next_ref = bf16[8,3,72,192]{3,2,1,0:T(8,128)(2,1)S(1)} collective-permute-done((bf16[8,3,72,192]{3,2,1,0:T(8,128)(2,1)S(1)}, bf16[8,3,72,192]{3,2,1,0:T(8,128)(2,1)S(1)}, u32[]{:S(2)}, u32[]{:S(2)}) %collective-permute-start.1) | collective-permute-done | bytes 663584 | tf_op jit(solution)/shard_map/ppermute | solution.py:299
  31.1 0.0 copy-start.9
  31.1 0.0 collective-permute-done.prev_ref
  31.1 0.0 copy-start.10
  31.1 1.0 pad_maximum_fusion
  32.1 0.0 collective-permute-start.2
  32.1 0.1 copy-done.10
  32.2 0.0 copy-start.3
  32.2 0.0 copy-start.5
  32.2 0.8 pad_maximum_fusion.1
  33.1 4.0 %collective-permute-start.3 = (bf16[8,12,8,192]{3,2,1,0:T(8,128)(2,1)}, bf16[8,12,8,192]{3,2,1,0:T(8,128)(2,1)S(1)}, u32[]{:S(2)}, u32[]{:S(2)}) collective-permute-start(bf16[8,12,8,192]{3,2,1,0:T(8,128)(2,1)} %pad_maximum_fusion.1), channel_id=1, source_target_pairs={{1,0},{2,1},{3,2},{4,3},{5,4},{6,5},{7,6},{0,7},{9,8},{10,9},{11,1... | collective-permute-start | bytes 884744 | tf_op jit(solution)/shard_map/ppermute | solution.py:299
  37.1 0.0 copy-done.12
  37.1 0.9 copy.20.wdown_ref
  38.0 0.0 copy-done.2
  38.0 0.0 copy-done.4
  38.0 0.0 copy-done.6
  38.0 10.4 %shard_map.164.bias1_ref = f32[4,2,144,256]{3,2,1,0:T(8,128)S(1)} custom-call(s32[1]{0:T(128)} %bitcast.1.cut_ref, f32[1,4,6,3312]{3,2,1,0:T(8,128)S(1)} %copy.18.table_ref, s32[144,144]{1,0:T(8,128)S(1)} %copy-done.2, bf16[3,48,144]{2,1,0:T(8,128)(2,1)S(1)} %copy-done.6, bf16[2,3,144,128]{3,2,1,0:T(8,128)(2,1)S(1)} %copy-done.4), custom_call_target="tpu_custom_call" | custom-call | tf_op jit(solution)/shard_map/pallas_call | solution.py:166
  48.4 0.0 copy-done.9
  48.4 0.0 copy-start
  48.4 1.0 copy-done
  49.5 0.0 collective-permute-done.4.table_ref
  49.5 0.0 copy-done.3
  49.5 0.0 copy-done.5
  49.5 10.4 %shard_map.163.bias0_ref = f32[4,2,144,256]{3,2,1,0:T(8,128)S(1)} custom-call(s32[1]{0:T(128)} %bitcast.cut_ref, f32[1,4,6,3312]{3,2,1,0:T(8,128)S(1)} %collective-permute-done.4.table_ref, s32[144,144]{1,0:T(8,128)S(1)} %copy-done.2, bf16[3,48,144]{2,1,0:T(8,128)(2,1)S(1)} %copy-done.5, bf16[2,3,144,128]{3,2,1,0:T(8,128)(2,1)S(1)} %copy-done.3), custom_call_target="tpu_custom_call" | custom-call | tf_op jit(solution)/shard_map/pallas_call | solution.py:166
  59.9 0.0 copy-start.1
  59.9 1.0 copy-done.1
  60.9 0.0 collective-permute-done.2.lo_ref.lh_ref
  60.9 0.0 copy-start.7
  60.9 0.0 collective-permute-done.3.ro_ref.rh_ref
  60.9 0.0 copy-start.8
  60.9 0.7 copy-done.7
  61.6 0.2 copy-done.8
  61.8 48.3 %shard_map.165 = bf16[8,6,72,192]{3,2,1,0:T(8,128)(2,1)} custom-call(bf16[8,6,72,192]{3,2,1,0:T(8,128)(2,1)} %own_ref.1, bf16[8,3,72,192]{3,2,1,0:T(8,128)(2,1)} %copy-done.10, bf16[8,3,72,192]{3,2,1,0:T(8,128)(2,1)} %copy-done.9, bf16[8,12,8,192]{3,2,1,0:T(8,128)(2,1)} %copy-done.7, bf16[8,12,8,192]{3,2,1,0:T(8,128)(2,1)} %copy-done.7, ...), custom_call_target="tpu_custom_call" | custom-call | tf_op jit(solution)/shard_map/pallas_call | solution.py:266
  (2 shorter events, 0.0 us)
Async XLA Ops:
  0.0 6.9 %copy-start.11 = (f32[1,4,6,3312]{3,1,2,0:T(4,128)S(1)}, f32[1,4,6,3312]{3,1,2,0:T(4,128)}, u32[]{:S(2)}) copy-start(f32[1,4,6,3312]{3,1,2,0:T(4,128)} %param.18) | copy-start | bytes 953860
  1.6 29.5 %collective-permute-start.1 = (bf16[8,3,72,192]{3,2,1,0:T(8,128)(2,1)S(1)}, bf16[8,3,72,192]{3,2,1,0:T(8,128)(2,1)S(1)}, u32[]{:S(2)}, u32[]{:S(2)}) collective-permute-start(bf16[8,3,72,192]{3,2,1,0:T(8,128)(2,1)S(1)} %get-tuple-element.7), channel_id=1, source_target_pairs={{8,0},{16,8},{24,16},{32,24},{40,32},{48,40},{56,48},{64,56},{72,6... | collective-permute-start | bytes 1990664 | tf_op jit(solution)/shard_map/ppermute | solution.py:299
  6.9 24.2 %collective-permute-start = (bf16[8,3,72,192]{3,2,1,0:T(8,128)(2,1)S(1)}, bf16[8,3,72,192]{3,2,1,0:T(8,128)(2,1)S(1)}, u32[]{:S(2)}, u32[]{:S(2)}) collective-permute-start(bf16[8,3,72,192]{3,2,1,0:T(8,128)(2,1)S(1)} %get-tuple-element.8), channel_id=1, source_target_pairs={{120,0},{0,8},{8,16},{16,24},{24,32},{32,40},{40,48},{48,56},{56,6... | collective-permute-start | bytes 1990664 | tf_op jit(solution)/shard_map/ppermute | solution.py:299
  7.0 30.1 %copy-start.12 = (bf16[768,192]{0,1:T(8,128)(2,1)S(1)}, bf16[768,192]{0,1:T(8,128)(2,1)}, u32[]{:S(2)}) copy-start(bf16[768,192]{0,1:T(8,128)(2,1)} %param.25) | copy-start | bytes 884740
  7.0 31.0 %copy-start.2 = (s32[144,144]{1,0:T(8,128)S(1)}, s32[144,144]{1,0:T(8,128)}, u32[]{:S(2)}) copy-start(s32[144,144]{1,0:T(8,128)} %index_ref.3) | copy-start | bytes 248836
  7.0 31.0 %copy-start.4 = (bf16[2,3,144,128]{3,2,1,0:T(8,128)(2,1)S(1)}, bf16[2,3,144,128]{3,2,1,0:T(8,128)(2,1)}, u32[]{:S(2)}) copy-start(bf16[2,3,144,128]{3,2,1,0:T(8,128)(2,1)} %constant.27.clone.lanes_ref) | copy-start | bytes 663556
  7.0 31.0 %copy-start.6 = (bf16[3,48,144]{2,1,0:T(8,128)(2,1)S(1)}, bf16[3,48,144]{2,1,0:T(8,128)(2,1)}, u32[]{:S(2)}) copy-start(bf16[3,48,144]{2,1,0:T(8,128)(2,1)} %constant.26.clone.keys_ref) | copy-start | bytes 124420
  7.0 42.5 %collective-permute-start.4 = (f32[1,4,6,3312]{3,2,1,0:T(8,128)S(1)}, f32[1,4,6,3312]{3,2,1,0:T(8,128)S(1)}, u32[]{:S(2)}, u32[]{:S(2)}) collective-permute-start(f32[1,4,6,3312]{3,2,1,0:T(8,128)S(1)} %copy.18.table_ref), channel_id=1, source_target_pairs={{120,0},{0,8},{8,16},{16,24},{24,32},{32,40},{40,48},{48,56},{56,6... | collective-permute-start | bytes 953864 | tf_op jit(solution)/shard_map/ppermute | solution.py:299
  31.1 17.4 %copy-start.9 = (bf16[8,3,72,192]{3,2,1,0:T(8,128)(2,1)}, bf16[8,3,72,192]{3,2,1,0:T(8,128)(2,1)S(1)}, u32[]{:S(2)}) copy-start(bf16[8,3,72,192]{3,2,1,0:T(8,128)(2,1)S(1)} %collective-permute-done.1.next_ref) | copy-start | bytes 1990660
  31.1 1.1 %copy-start.10 = (bf16[8,3,72,192]{3,2,1,0:T(8,128)(2,1)}, bf16[8,3,72,192]{3,2,1,0:T(8,128)(2,1)S(1)}, u32[]{:S(2)}) copy-start(bf16[8,3,72,192]{3,2,1,0:T(8,128)(2,1)S(1)} %collective-permute-done.prev_ref) | copy-start | bytes 1990660
  32.1 28.8 %collective-permute-start.2 = (bf16[8,12,8,192]{3,2,1,0:T(8,128)(2,1)}, bf16[8,12,8,192]{3,2,1,0:T(8,128)(2,1)S(1)}, u32[]{:S(2)}, u32[]{:S(2)}) collective-permute-start(bf16[8,12,8,192]{3,2,1,0:T(8,128)(2,1)} %pad_maximum_fusion), channel_id=1, source_target_pairs={{7,0},{0,1},{1,2},{2,3},{3,4},{4,5},{5,6},{6,7},{15,8},{8,9},{9,10... | collective-permute-start | bytes 884744 | tf_op jit(solution)/shard_map/ppermute | solution.py:299
  32.2 17.3 %copy-start.3 = (bf16[2,3,144,128]{3,2,1,0:T(8,128)(2,1)S(1)}, bf16[2,3,144,128]{3,2,1,0:T(8,128)(2,1)}, u32[]{:S(2)}) copy-start(bf16[2,3,144,128]{3,2,1,0:T(8,128)(2,1)} %constant.29.clone.lanes_ref) | copy-start | bytes 663556
  32.2 17.3 %copy-start.5 = (bf16[3,48,144]{2,1,0:T(8,128)(2,1)S(1)}, bf16[3,48,144]{2,1,0:T(8,128)(2,1)}, u32[]{:S(2)}) copy-start(bf16[3,48,144]{2,1,0:T(8,128)(2,1)} %constant.28.clone.keys_ref) | copy-start | bytes 124420
  33.1 27.8 %collective-permute-start.3 = (bf16[8,12,8,192]{3,2,1,0:T(8,128)(2,1)}, bf16[8,12,8,192]{3,2,1,0:T(8,128)(2,1)S(1)}, u32[]{:S(2)}, u32[]{:S(2)}) collective-permute-start(bf16[8,12,8,192]{3,2,1,0:T(8,128)(2,1)} %pad_maximum_fusion.1), channel_id=1, source_target_pairs={{1,0},{2,1},{3,2},{4,3},{5,4},{6,5},{7,6},{0,7},{9,8},{10,9},{11,1... | collective-permute-start | bytes 884744 | tf_op jit(solution)/shard_map/ppermute | solution.py:299
  48.4 1.0 copy-start
  59.9 1.0 copy-start.1
  60.9 0.8 copy-start.7
  60.9 0.9 copy-start.8

commit v2 on v1

v2 whole, which is shorter than its diff:
```python
import jax
import jax.numpy as jnp
import numpy as np
from jax import lax
from jax.experimental import pallas as pl
from jax.experimental.pallas import tpu as pltpu
from jax.sharding import PartitionSpec as P

HEADS = 6
HD = 32
C = 192
FFH = 768
ZW = 4
COLS = 72
UNITS = 12
WINS = 7
SLOT = 40
NEG = -1e30
LOG2E = 1.4426950408889634
EPS = 1e-05
F32 = jnp.float32
BF16 = jnp.bfloat16
GELU = (0.7978822019334538, 0.03634471964715062, -4.492210425823531e-05,
        -5.034912992251254e-05, 3.0967343436505324e-06, -6.630250880453595e-08)


def head_row(h):
    return h * SLOT + (8 if h >= 3 else 0)


def unit_place(c):
    return (c + 1) // 2, (c + 1) % 2


def gather_maps():
    perm = np.zeros((504, 432), np.float32)
    left = np.zeros((72, 48), np.float32)
    right = np.zeros((72, 48), np.float32)
    back = np.zeros((432, 480), np.float32)
    for c in range(-1, 13):
        m, half = unit_place(c)
        for r in range(6):
            for j in range(6):
                row = 72 * m + 36 * half + r * 6 + j
                if c == -1:
                    left[row, r * 8 + 2 + j] = 1
                elif c == 12:
                    right[row - 432, r * 8 + j] = 1
                else:
                    perm[row, r * COLS + 6 * c + j] = 1
                    back[r * COLS + 6 * c + j, c * SLOT + 4 * half + r * 6 + j] = 1
    return [x.astype(jnp.bfloat16) for x in (perm, left, right, back)]


def key_position(latw, key):
    halo, rest = divmod(key, 72)
    half, rest = divmod(rest, 36)
    dz, rest = divmod(rest, 18)
    di, j = divmod(rest, 6)
    upper = (latw == 0) == (halo == 0)
    return (dz * 6 + di + (3 if upper else 0)) * 12 + 6 * half + j


def index_maps():
    keys = np.zeros((2, 3, 48, 144), np.float32)
    lanes = np.zeros((2, 2, 3, 144, 128), np.float32)
    for latw in range(2):
        for key in range(144):
            keys[latw, key // 48, key % 48, key_position(latw, key)] = 1
        for half in range(2):
            for s in range(36):
                pos = key_position(latw, 36 * half + s)
                for third in range(3):
                    lanes[latw, half, third, pos, third * SLOT + 4 * half + s] = 1
    return keys.astype(jnp.bfloat16), lanes.astype(jnp.bfloat16)


def nt(a, b):
    return lax.dot_general(a, b, (((1,), (1,)), ((), ())), preferred_element_type=F32)


def tn(a, b):
    return lax.dot_general(a, b, (((0,), (0,)), ((), ())), preferred_element_type=F32)


def nn(a, b):
    return jnp.dot(a, b, preferred_element_type=F32)


POS = 3312
CH = 13


def bias_kernel(cut_ref, table_ref, index_ref, keys_ref, lanes_ref, out_ref, thi, tlo, lo_s, hi_s, g_s):
    for ch in range(CH):
        width = min(256, POS - 256 * ch)
        rows = jnp.concatenate([table_ref[0, z, :, 256 * ch : 256 * ch + width] for z in range(ZW)], axis=0)
        if width < 256:
            rows = jnp.concatenate([rows, jnp.zeros((24, 256 - width), F32)], axis=1)
        rows = rows * LOG2E
        top = rows.astype(BF16).astype(F32)
        thi[24 * ch : 24 * ch + 24] = top
        tlo[24 * ch : 24 * ch + 24] = rows - top
    index = index_ref[...]
    index_lo = (index & 255).astype(F32).astype(BF16)
    index_hi = (index >> 8).astype(F32).astype(BF16)
    for half in range(2):
        for part, dst in ((index_lo, lo_s), (index_hi, hi_s)):
            total = jnp.zeros((48, 128), F32)
            for third in range(3):
                rows = nt(keys_ref[third], part).astype(BF16)
                total = total + nn(rows, lanes_ref[half, third])
            dst[48 * half : 48 * half + 48] = total.astype(jnp.int32)
    top = thi[...].astype(BF16)
    low = tlo[...].astype(BF16)
    both = jnp.concatenate([top, low], axis=0)
    spread = lax.broadcasted_iota(jnp.int32, (256, 128), 0).astype(F32).astype(BF16)

    def step(i, _):
        lo = lo_s[pl.ds(i, 1), :]
        hi = hi_s[pl.ds(i, 1), :]
        lo2 = lo_s[pl.ds(i + 48, 1), :]
        hi2 = hi_s[pl.ds(i + 48, 1), :]
        hot = jnp.concatenate(
            [jnp.where(spread == v.astype(F32).astype(BF16), BF16(1), BF16(0)) for v in (lo, lo2)], axis=1
        )
        vals = nn(both, hot)
        vals = vals[: 24 * CH] + vals[24 * CH :]
        his = jnp.concatenate([hi, hi2], axis=1)
        his = jnp.broadcast_to(his, (24, 256))
        acc = vals[0:24]
        for ch in range(1, CH):
            acc = jnp.where(his == ch, vals[24 * ch : 24 * ch + 24], acc)
        g_s[i] = acc
        return 0

    lax.fori_loop(0, 48, step, 0, unroll=8)
    lane = lax.broadcasted_iota(jnp.int32, (8, 128), 1)
    cut = cut_ref[0] == 1
    sub = lax.broadcasted_iota(jnp.int32, (144, 1), 0)

    def arrange(z, _):
        for half in range(2):
            for tile in range(2):
                for k8 in range(6):
                    three = [
                        g_s[pl.ds(8 * k8, 8), z * HEADS + 3 * tile + h, 128 * half : 128 * half + 128]
                        for h in range(3)
                    ]
                    for third in range(3):
                        moved = [
                            three[h] if h == third else pltpu.roll(three[h], (SLOT * (h - third)) % 128, 1)
                            for h in range(3)
                        ]
                        got = jnp.where(lane < SLOT, moved[0], jnp.where(lane < 2 * SLOT, moved[1], moved[2]))
                        row = 48 * third + 8 * k8
                        if row >= 72:
                            got = jnp.where(cut, NEG, got)
                        out_ref[z, half, row : row + 8, 128 * tile : 128 * tile + 128] = got
        return 0

    for z in range(ZW):
        arrange(z, 0)


def make_bias(cut, table, index_table, keys, lanes):
    return pl.pallas_call(
        bias_kernel,
        out_shape=jax.ShapeDtypeStruct((ZW, 2, 144, 256), F32),
        in_specs=[pl.BlockSpec(memory_space=pltpu.SMEM)] + [pl.BlockSpec(memory_space=pltpu.VMEM)] * 4,
        out_specs=pl.BlockSpec(memory_space=pltpu.VMEM),
        scratch_shapes=[
            pltpu.VMEM((24 * CH, 256), F32),
            pltpu.VMEM((24 * CH, 256), F32),
            pltpu.VMEM((96, 128), jnp.int32),
            pltpu.VMEM((96, 128), jnp.int32),
            pltpu.VMEM((48, 24, 256), F32),
        ],
        compiler_params=pltpu.CompilerParams(vmem_limit_bytes=16 * 2**20),
        cost_estimate=pl.CostEstimate(flops=8 * 10**9, bytes_accessed=2 * 10**6, transcendentals=0),
    )(cut, table, index_table, keys, lanes)


def packed_shape(levels, rows, cols):
    return jax.ShapeDtypeStruct((3 * levels // 2, rows, cols, 128), BF16)


def pack(dst, x):
    levels = x.shape[0]
    dst[:levels] = x[..., :128]
    for i in range(levels // 2):
        dst[levels + i] = jnp.concatenate([x[2 * i, ..., 128:], x[2 * i + 1, ..., 128:]], axis=-1)


def unpack(src, levels, z):
    low = src[pl.ds(2 * z, 2)].astype(F32)
    high = src[pl.ds(levels + z, 1)].astype(F32)
    rows = low.shape[1] * low.shape[2]
    low = low.reshape(2, rows, 128)
    high = high.reshape(rows, 128)
    parts = [jnp.concatenate([low[dz], high[:, 64 * dz : 64 * dz + 64]], axis=1) for dz in range(2)]
    return jnp.concatenate(parts, axis=0).astype(BF16)


def pack_kernel(x_ref, up, dn, er, el):
    pack(up, x_ref[:, 3:6])
    pack(dn, x_ref[:, 0:3])
    pack(er, x_ref[:, :, COLS - 8 :])
    pack(el, x_ref[:, :, :8])


def make_packs(tokens):
    vmem = pl.BlockSpec(memory_space=pltpu.VMEM)
    shapes = [packed_shape(8, 3, COLS)] * 2 + [packed_shape(8, 6, 8)] * 2
    return pl.pallas_call(
        pack_kernel,
        out_shape=shapes,
        in_specs=[vmem],
        out_specs=[vmem] * len(shapes),
        compiler_params=pltpu.CompilerParams(vmem_limit_bytes=16 * 2**20),
    )(tokens)


def rim_kernel(l_ref, r_ref, up, dn):
    for side, ref in enumerate((l_ref, r_ref)):
        up[side] = ref[:, 3:6]
        dn[side] = ref[:, 0:3]


def make_rims(left, right):
    vmem = pl.BlockSpec(memory_space=pltpu.VMEM)
    shape = jax.ShapeDtypeStruct((2, 12, 3, 8, 128), BF16)
    return pl.pallas_call(rim_kernel, out_shape=[shape] * 2, in_specs=[vmem] * 2, out_specs=[vmem] * 2)(left, right)


def block_kernel(own_ref, prev_ref, next_ref, l_ref, r_ref, cp_ref, cn_ref, bias0_ref, bias1_ref,
                 ga_ref, wqkv_ref, wproj_ref, gm_ref, wup_ref, wdown_ref,
                 perm_ref, left_ref, right_ref, back_ref, out_ref,
                 xs, ns, qs, kvs, os_, rs, ob, ss, ps, sems):
    def flat(v):
        return v.astype(F32).reshape(-1, C).astype(BF16)

    ones = jnp.ones((C, 128), BF16)
    gain = ga_ref[...]
    lane = lax.broadcasted_iota(jnp.int32, (SLOT, C), 1) // HD
    pad = jnp.zeros((8, C), F32)

    def both(v):
        return jnp.concatenate([v, v[:, : C - 128]], axis=1)

    def half_row(z, latw):
        levels = pl.ds(2 * z, 2)
        row = 3 * latw
        own = flat(own_ref[levels, row : row + 3])
        halo = unpack(next_ref if latw else prev_ref, 8, z)
        bias_ref = bias1_ref if latw else bias0_ref
        perm = perm_ref[...]
        own_edges = [unpack(e.at[:, row : row + 3], 8, z) for e in (l_ref, r_ref)]
        halo_edges = [unpack((cn_ref if latw else cp_ref).at[side], 8, z) for side in range(2)]
        for base, block, edges in ((0, own, own_edges), (72, halo, halo_edges)):
            got = nn(perm, block)
            edge_l = nn(left_ref[...], edges[0])
            edge_r = nn(right_ref[...], edges[1])
            for m in range(WINS):
                piece = got[72 * m : 72 * m + 72]
                if m == 0:
                    piece = piece + edge_l
                if m == WINS - 1:
                    piece = piece + edge_r
                xs[144 * m + base : 144 * m + base + 72] = piece
        for m in range(WINS):
            x = xs[144 * m : 144 * m + 144]
            mean = both(nn(x.astype(BF16), ones) * (1.0 / C))
            cen = x - mean
            var = nn((cen * cen).astype(BF16), ones) * (1.0 / C)
            inv = both(lax.rsqrt(var + EPS))
            ns[144 * m : 144 * m + 144] = (cen * inv * gain).astype(BF16)
        packed = nn(ns[...], wqkv_ref[...])
        qs[...] = packed[:, :C] * (HD ** -0.5 * LOG2E)
        kvs[...] = packed[:, C:].astype(BF16)
        def scores(c):
            m, half = unit_place(c)
            q = qs[144 * m + 32 * half : 144 * m + 32 * half + SLOT]
            rows = []
            for h in range(HEADS):
                rows.append(jnp.where(lane == h, q, 0.0))
                if h in (2, 5):
                    rows.append(pad)
            qm = jnp.concatenate(rows, axis=0).astype(BF16)
            return nt(kvs[144 * m : 144 * m + 144, :C], qm) + bias_ref[z, half]

        def soft(s):
            e = jnp.exp2(s - jnp.max(s, axis=0, keepdims=True))
            return (e * (1.0 / jnp.sum(e, axis=0, keepdims=True))).astype(BF16)

        def attend(c, p):
            m, half = unit_place(c)
            o = tn(p, kvs[144 * m : 144 * m + 144, C:])
            out = o[0:SLOT]
            for h in range(1, HEADS):
                out = jnp.where(lane == h, o[head_row(h) : head_row(h) + SLOT], out)
            os_[SLOT * c : SLOT * c + SLOT] = out
            rs[SLOT * c : SLOT * c + SLOT] = xs[144 * m + 32 * half : 144 * m + 32 * half + SLOT]

        for c in range(UNITS):
            ss[c] = scores(c)
        for c in range(UNITS):
            ps[c] = soft(ss[c])
        for c in range(UNITS):
            attend(c, ps[c])
        resid = rs[...] + nn(os_[...].astype(BF16), wproj_ref[...])
        mean = jnp.mean(resid, axis=1, keepdims=True)
        cen = resid - mean
        var = nn((cen * cen).astype(BF16), ones) * (1.0 / C)
        normed = (cen * both(lax.rsqrt(var + EPS)) * gm_ref[...]).astype(BF16)
        u = nn(normed, wup_ref[...])
        w = jnp.minimum(u * u, 25.0)
        poly = jnp.full_like(w, GELU[-1])
        for coef in GELU[-2::-1]:
            poly = poly * w + coef
        hidden = (u + u * jnp.tanh(u * poly)).astype(BF16)
        out = (resid + 0.5 * nn(hidden, wdown_ref[...])).astype(BF16)
        ob[z, :, row : row + 3] = nn(back_ref[...], out).reshape(2, 3, COLS, C).astype(BF16)

    def leave(z):
        return pltpu.make_async_copy(ob.at[z], out_ref.at[pl.ds(2 * z, 2)], sems.at[z])

    def step(z, _):
        for latw in range(2):
            half_row(z, latw)
        leave(z).start()
        return 0

    lax.fori_loop(0, ZW, step, 0)
    for z in range(ZW):
        leave(z).wait()


def run_block(tokens, halos, edges, biases, weights, maps):
    vmem = pl.BlockSpec(memory_space=pltpu.VMEM)
    operands = (tokens, *halos, *edges, *biases, *weights, *maps)
    return pl.pallas_call(
        block_kernel,
        out_shape=jax.ShapeDtypeStruct(tokens.shape, BF16),
        in_specs=[vmem] * len(operands),
        out_specs=pl.BlockSpec(memory_space=pl.ANY),
        scratch_shapes=[
            pltpu.VMEM((1008, C), F32),
            pltpu.VMEM((1008, C), BF16),
            pltpu.VMEM((1008, C), F32),
            pltpu.VMEM((1008, 2 * C), BF16),
            pltpu.VMEM((480, C), F32),
            pltpu.VMEM((480, C), F32),
            pltpu.VMEM((ZW, 2, 6, COLS, C), BF16),
            pltpu.VMEM((UNITS, 144, 256), F32),
            pltpu.VMEM((UNITS, 144, 256), BF16),
            pltpu.SemaphoreType.DMA((ZW,)),
        ],
        compiler_params=pltpu.CompilerParams(vmem_limit_bytes=24 * 2**20),
        cost_estimate=pl.CostEstimate(flops=30 * 10**9, bytes_accessed=2 * 10**6, transcendentals=0),
    )(*operands)


def passed_along(block, lat, lon):
    nlat, nlon = lax.axis_size("lat"), lax.axis_size("lon")
    route = [
        (((i - lat) % nlat) * nlon + (j - lon) % nlon, i * nlon + j) for i in range(nlat) for j in range(nlon)
    ]
    return lax.ppermute(block, ("lat", "lon"), route)


def shards(tokens, bias_table, index_table, gain_attn, w_qkv, w_proj, gain_mlp, w_up, w_down):
    place = lax.axis_index("lat")
    last = lax.axis_size("lat") - 1
    up, dn, er, el = make_packs(tokens)
    prev_table = passed_along(bias_table.reshape(-1, 128), 1, 0).reshape(bias_table.shape)
    halos = (passed_along(up, 1, 0), passed_along(dn, -1, 0))
    left, right = passed_along(er, 0, 1), passed_along(el, 0, -1)
    rim_up, rim_dn = make_rims(left, right)
    edges = (left, right, passed_along(rim_up, 1, 0), passed_along(rim_dn, -1, 0))
    keys, lanes = index_maps()
    maps = gather_maps()
    cut1 = (place == last).astype(jnp.int32).reshape(1)
    cut0 = (place == 0).astype(jnp.int32).reshape(1)
    bias1 = make_bias(cut1, bias_table, index_table, keys[1], lanes[1])
    bias0 = make_bias(cut0, prev_table, index_table, keys[0], lanes[0])
    weights = (gain_attn.reshape(1, C), w_qkv, w_proj, gain_mlp.reshape(1, C), w_up, w_down)
    return run_block(tokens, halos, edges, (bias0, bias1), weights, maps)


def solution(mesh):
    return jax.shard_map(
        shards,
        mesh=mesh,
        in_specs=(
            P(None, "lat", "lon", None),
            P("lat", None, None, None),
            P(),
            P(),
            P(),
            P(),
            P(),
            P(),
            P(),
        ),
        out_specs=P(None, "lat", "lon", None),
        check_vma=False,
    )
```

time: 110 us -> 75.7 us (0.69)
  the two profiles are of different devices: /device:TPU:8 before, /device:TPU:0 now
where the time goes in v2:
time: 75.7 us; the launch traced here: 75.3 us
  Pallas kernels  49.5 us (65%)
  starting transfers between devices  15.2 us (20%)
  local copies, waits for them, and re-layouts  10.1 us (13%)
    pallas_call x1, Pallas kernels, run_block(): pl.pallas_call(block_kernel, out_shape=jax.ShapeDtypeStruct(tokens.shape,...  34.1 us
    ppermute x7, starting transfers between devices, passed_along(): return lax.ppermute(block, ('lat', 'lon'), route)  15.2 us
    pallas_call x2, Pallas kernels, make_bias(): pl.pallas_call(bias_kernel, out_shape=jax.ShapeDtypeStruct((ZW, 2, 144, 2...  13.3 us
    unnamed x46, local copies, waits for them, and re-layouts  7.91 us
    pallas_call x1, Pallas kernels, make_rims(): pl.pallas_call(rim_kernel, out_shape=[shape] * 2, in_specs=[vmem] * 2, ou...  1.75 us
  transfers between devices with their start and end apart: 7, of which 0 were waited for; matrix products, arithmetic and copies ran while one was open for 3% of the time, Pallas kernels for 20%

profile of v2, /device:TPU:0, one launch (start us, length us, event | category | flops | bytes accessed | tf_op | source)
XLA Modules:
  0.0 75.3 jit_solution(13930591220950260222)
XLA Ops:
  0.0 1.1 %copy.20.table_ref = f32[1,4,6,3312]{3,2,1,0:T(8,128)S(1)} copy(f32[1,4,6,3312]{3,1,2,0:T(4,128)} %param.18) | data formatting | bytes 635904 | tf_op args[1]
  1.1 0.9 %reshape.24 = f32[621,128]{1,0:T(8,128)} reshape(f32[1,4,6,3312]{3,2,1,0:T(8,128)S(1)} %copy.20.table_ref) | data formatting | bytes 635904 | tf_op jit(solution)/shard_map/reshape | solution.py:376
  2.1 0.0 collective-permute-start.6
  2.1 1.5 %copy-done = bf16[8,6,72,192]{3,2,1,0:T(8,128)(2,1)S(1)} copy-done((bf16[8,6,72,192]{3,2,1,0:T(8,128)(2,1)S(1)}, bf16[8,6,72,192]{3,2,1,0:T(8,128)(2,1)}, u32[]{:S(2)}) %copy-start) | copy-done | bytes 1327128
  3.5 0.4 shard_map.163
  3.9 1.6 %collective-permute-start.2 = (bf16[12,6,8,128]{3,2,1,0:T(8,128)(2,1)S(1)}, bf16[12,6,8,128]{3,2,1,0:T(8,128)(2,1)S(1)}, u32[]{:S(2)}, u32[]{:S(2)}) collective-permute-start(bf16[12,6,8,128]{3,2,1,0:T(8,128)(2,1)S(1)} %get-tuple-element.13), channel_id=1, source_target_pairs={{7,0},{0,1},{1,2},{2,3},{3,4},{4,5},{5,6},{6,7},{15,8},{8,9},{9,10... | collective-permute-start | bytes 442376 | tf_op jit(solution)/shard_map/ppermute | solution.py:369
  5.5 2.6 %collective-permute-start.3 = (bf16[12,6,8,128]{3,2,1,0:T(8,128)(2,1)S(1)}, bf16[12,6,8,128]{3,2,1,0:T(8,128)(2,1)S(1)}, u32[]{:S(2)}, u32[]{:S(2)}) collective-permute-start(bf16[12,6,8,128]{3,2,1,0:T(8,128)(2,1)S(1)} %get-tuple-element.14), channel_id=1, source_target_pairs={{1,0},{2,1},{3,2},{4,3},{5,4},{6,5},{7,6},{0,7},{9,8},{10,9},{11,1... | collective-permute-start | bytes 442376 | tf_op jit(solution)/shard_map/ppermute | solution.py:369
  8.1 2.8 %collective-permute-start = (bf16[12,3,72,128]{3,2,1,0:T(8,128)(2,1)S(1)}, bf16[12,3,72,128]{3,2,1,0:T(8,128)(2,1)S(1)}, u32[]{:S(2)}, u32[]{:S(2)}) collective-permute-start(bf16[12,3,72,128]{3,2,1,0:T(8,128)(2,1)S(1)} %get-tuple-element.11), channel_id=1, source_target_pairs={{120,0},{121,1},{122,2},{123,3},{124,4},{125,5},{126,6},{127,7},{0... | collective-permute-start | bytes 1990664 | tf_op jit(solution)/shard_map/ppermute | solution.py:369
  10.9 2.8 %collective-permute-start.1 = (bf16[12,3,72,128]{3,2,1,0:T(8,128)(2,1)S(1)}, bf16[12,3,72,128]{3,2,1,0:T(8,128)(2,1)}, u32[]{:S(2)}, u32[]{:S(2)}) collective-permute-start(bf16[12,3,72,128]{3,2,1,0:T(8,128)(2,1)S(1)} %get-tuple-element.12), channel_id=1, source_target_pairs={{8,0},{9,1},{10,2},{11,3},{12,4},{13,5},{14,6},{15,7},{16,8},{17,9... | collective-permute-start | bytes 1990664 | tf_op jit(solution)/shard_map/ppermute | solution.py:369
  13.7 0.0 copy-done.15
  13.7 0.0 copy-done.17
  13.8 0.0 copy-done.8
  13.8 6.6 %shard_map.166.bias1_ref = f32[4,2,144,256]{3,2,1,0:T(8,128)S(1)} custom-call(s32[1]{0:T(128)} %bitcast.1.cut_ref, f32[1,4,6,3312]{3,2,1,0:T(8,128)S(1)} %copy.20.table_ref, s32[144,144]{1,0:T(8,128)S(1)} %copy-done.8, bf16[3,48,144]{2,1,0:T(8,128)(2,1)S(1)} %copy-done.17, bf16[2,3,144,128]{3,2,1,0:T(8,128)(2,1)S(1)} %copy-done.15), custom_call_target="tpu_custom_call" | custom-call | flops 8000000000 | bytes 2000000 | tf_op jit(solution)/shard_map/pallas_call | solution.py:167
  20.4 0.0 copy-start.20
  20.4 1.0 %copy-done.20 = f32[4,2,144,256]{3,2,1,0:T(8,128)} copy-done((f32[4,2,144,256]{3,2,1,0:T(8,128)}, f32[4,2,144,256]{3,2,1,0:T(8,128)S(1)}, u32[]{:S(2)}) %copy-start.20) | copy-done | bytes 1179672
  21.4 1.1 %copy.22.wdown_ref = bf16[768,192]{1,0:T(8,128)(2,1)S(1)} copy(bf16[768,192]{0,1:T(8,128)(2,1)} %param.25) | data formatting | bytes 589824 | tf_op args[8]
  22.6 0.0 collective-permute-done.2.l_ref
  22.6 0.0 copy-start.2
  22.6 0.0 collective-permute-done.3.r_ref
  22.6 0.6 copy-done.2
  23.2 0.7 copy-done.4
  23.9 1.8 %shard_map.164 = (bf16[2,12,3,8,128]{4,3,2,1,0:T(8,128)(2,1)}, bf16[2,12,3,8,128]{4,3,2,1,0:T(8,128)(2,1)}) custom-call(bf16[12,6,8,128]{3,2,1,0:T(8,128)(2,1)} %copy-done.2, bf16[12,6,8,128]{3,2,1,0:T(8,128)(2,1)} %copy-done.4), custom_call_target="tpu_custom_call" | custom-call | tf_op jit(solution)/shard_map/pallas_call | solution.py:233
  25.6 0.0 collective-permute-start.4
  25.6 5.4 %collective-permute-start.5 = (bf16[2,12,3,8,128]{4,3,2,1,0:T(8,128)(2,1)}, bf16[2,12,3,8,128]{4,3,2,1,0:T(8,128)(2,1)S(1)}, u32[]{:S(2)}, u32[]{:S(2)}) collective-permute-start(bf16[2,12,3,8,128]{4,3,2,1,0:T(8,128)(2,1)} %get-tuple-element.16), channel_id=1, source_target_pairs={{8,0},{9,1},{10,2},{11,3},{12,4},{13,5},{14,6},{15,7},{16,8},{17,9... | collective-permute-start | bytes 442376 | tf_op jit(solution)/shard_map/ppermute | solution.py:369
  31.0 0.0 collective-permute-done.6
  31.0 1.3 %reshape.25.table_ref = f32[1,4,6,3312]{3,2,1,0:T(8,128)S(1)} reshape(f32[621,128]{1,0:T(8,128)} %collective-permute-done.6) | data formatting | bytes 635904 | tf_op jit(solution)/shard_map/reshape | solution.py:376
  32.3 0.0 copy-start.14
  32.3 0.9 %copy-done.14 = bf16[2,3,144,128]{3,2,1,0:T(8,128)(2,1)S(1)} copy-done((bf16[2,3,144,128]{3,2,1,0:T(8,128)(2,1)S(1)}, bf16[2,3,144,128]{3,2,1,0:T(8,128)(2,1)}, u32[]{:S(2)}) %copy-start.14) | copy-done | bytes 221208
  33.2 0.9 %copy-done.16 = bf16[3,48,144]{2,1,0:T(8,128)(2,1)S(1)} copy-done((bf16[3,48,144]{2,1,0:T(8,128)(2,1)S(1)}, bf16[3,48,144]{2,1,0:T(8,128)(2,1)}, u32[]{:S(2)}) %copy-start.16) | copy-done | bytes 41496
  34.1 0.0 copy-start.7
  34.1 0.0 copy-start.9
  34.1 0.0 copy-start.10
  34.1 0.0 copy-start.11
  34.2 0.0 copy-start.12
  34.2 0.0 copy-start.13
  34.2 0.0 copy-start.18
  34.2 0.0 copy-start.19
  34.2 0.0 copy-start.21
  34.2 6.7 %shard_map.165.bias0_ref = f32[4,2,144,256]{3,2,1,0:T(8,128)S(1)} custom-call(s32[1]{0:T(128)} %bitcast.cut_ref, f32[1,4,6,3312]{3,2,1,0:T(8,128)S(1)} %reshape.25.table_ref, s32[144,144]{1,0:T(8,128)S(1)} %copy-done.8, bf16[3,48,144]{2,1,0:T(8,128)(2,1)S(1)} %copy-done.16, bf16[2,3,144,128]{3,2,1,0:T(8,128)(2,1)S(1)} %copy-done.14), custom_call_target="tpu_custom_call" | custom-call | flops 8000000000 | bytes 2000000 | tf_op jit(solution)/shard_map/pallas_call | solution.py:167
  40.9 0.0 collective-permute-done.4.cp_ref
  40.9 0.0 collective-permute-done.5.cn_ref
  40.9 0.0 collective-permute-done.prev_ref
  40.9 0.0 collective-permute-done.1.next_ref
  40.9 0.0 copy-done.1
  40.9 0.0 copy-done.3
  40.9 0.0 copy-done.5
  41.0 0.0 copy-done.6
  41.1 34.1 %shard_map.167 = bf16[8,6,72,192]{3,2,1,0:T(8,128)(2,1)} custom-call(bf16[8,6,72,192]{3,2,1,0:T(8,128)(2,1)S(1)} %copy-done.1, bf16[12,3,72,128]{3,2,1,0:T(8,128)(2,1)S(1)} %collective-permute-done.prev_ref, bf16[12,3,72,128]{3,2,1,0:T(8,128)(2,1)} %collective-permute-done.1.next_ref, bf16[12,6,8,128]{3,2,1,0:T(8,128)(2,1)S(1)} %copy-done.3, ...), custom_call_target="tpu_custom_call" | custom-call | flops 30000001024 | bytes 2000000 | tf_op jit(solution)/shard_map/pallas_call | solution.py:342
  (19 shorter events, 0.0 us)
Async XLA Ops:
  0.0 13.7 %copy-start.15 = (bf16[2,3,144,128]{3,2,1,0:T(8,128)(2,1)S(1)}, bf16[2,3,144,128]{3,2,1,0:T(8,128)(2,1)}, u32[]{:S(2)}) copy-start(bf16[2,3,144,128]{3,2,1,0:T(8,128)(2,1)} %constant.27.clone.lanes_ref) | copy-start | bytes 663556
  0.0 13.7 %copy-start.17 = (bf16[3,48,144]{2,1,0:T(8,128)(2,1)S(1)}, bf16[3,48,144]{2,1,0:T(8,128)(2,1)}, u32[]{:S(2)}) copy-start(bf16[3,48,144]{2,1,0:T(8,128)(2,1)} %constant.26.clone.keys_ref) | copy-start | bytes 124420
  0.0 13.7 %copy-start.8 = (s32[144,144]{1,0:T(8,128)S(1)}, s32[144,144]{1,0:T(8,128)}, u32[]{:S(2)}) copy-start(s32[144,144]{1,0:T(8,128)} %index_ref.3) | copy-start | bytes 248836
  2.1 28.9 %collective-permute-start.6 = (f32[621,128]{1,0:T(8,128)}, f32[621,128]{1,0:T(8,128)}, u32[]{:S(2)}, u32[]{:S(2)}) collective-permute-start(f32[621,128]{1,0:T(8,128)} %reshape.24), channel_id=1, source_target_pairs={{120,0},{121,1},{122,2},{123,3},{124,4},{125,5},{126,6},{127,7},{0... | collective-permute-start | bytes 953864 | tf_op jit(solution)/shard_map/ppermute | solution.py:369
  2.1 1.5 %copy-start = (bf16[8,6,72,192]{3,2,1,0:T(8,128)(2,1)S(1)}, bf16[8,6,72,192]{3,2,1,0:T(8,128)(2,1)}, u32[]{:S(2)}) copy-start(bf16[8,6,72,192]{3,2,1,0:T(8,128)(2,1)} %own_ref.1) | copy-start | bytes 3981316
  3.9 18.7 %collective-permute-start.2 = (bf16[12,6,8,128]{3,2,1,0:T(8,128)(2,1)S(1)}, bf16[12,6,8,128]{3,2,1,0:T(8,128)(2,1)S(1)}, u32[]{:S(2)}, u32[]{:S(2)}) collective-permute-start(bf16[12,6,8,128]{3,2,1,0:T(8,128)(2,1)S(1)} %get-tuple-element.13), channel_id=1, source_target_pairs={{7,0},{0,1},{1,2},{2,3},{3,4},{4,5},{5,6},{6,7},{15,8},{8,9},{9,10... | collective-permute-start | bytes 442376 | tf_op jit(solution)/shard_map/ppermute | solution.py:369
  5.5 17.0 %collective-permute-start.3 = (bf16[12,6,8,128]{3,2,1,0:T(8,128)(2,1)S(1)}, bf16[12,6,8,128]{3,2,1,0:T(8,128)(2,1)S(1)}, u32[]{:S(2)}, u32[]{:S(2)}) collective-permute-start(bf16[12,6,8,128]{3,2,1,0:T(8,128)(2,1)S(1)} %get-tuple-element.14), channel_id=1, source_target_pairs={{1,0},{2,1},{3,2},{4,3},{5,4},{6,5},{7,6},{0,7},{9,8},{10,9},{11,1... | collective-permute-start | bytes 442376 | tf_op jit(solution)/shard_map/ppermute | solution.py:369
  8.1 32.8 %collective-permute-start = (bf16[12,3,72,128]{3,2,1,0:T(8,128)(2,1)S(1)}, bf16[12,3,72,128]{3,2,1,0:T(8,128)(2,1)S(1)}, u32[]{:S(2)}, u32[]{:S(2)}) collective-permute-start(bf16[12,3,72,128]{3,2,1,0:T(8,128)(2,1)S(1)} %get-tuple-element.11), channel_id=1, source_target_pairs={{120,0},{121,1},{122,2},{123,3},{124,4},{125,5},{126,6},{127,7},{0... | collective-permute-start | bytes 1990664 | tf_op jit(solution)/shard_map/ppermute | solution.py:369
  10.9 30.0 %collective-permute-start.1 = (bf16[12,3,72,128]{3,2,1,0:T(8,128)(2,1)S(1)}, bf16[12,3,72,128]{3,2,1,0:T(8,128)(2,1)}, u32[]{:S(2)}, u32[]{:S(2)}) collective-permute-start(bf16[12,3,72,128]{3,2,1,0:T(8,128)(2,1)S(1)} %get-tuple-element.12), channel_id=1, source_target_pairs={{8,0},{9,1},{10,2},{11,3},{12,4},{13,5},{14,6},{15,7},{16,8},{17,9... | collective-permute-start | bytes 1990664 | tf_op jit(solution)/shard_map/ppermute | solution.py:369
  20.4 1.0 %copy-start.20 = (f32[4,2,144,256]{3,2,1,0:T(8,128)}, f32[4,2,144,256]{3,2,1,0:T(8,128)S(1)}, u32[]{:S(2)}) copy-start(f32[4,2,144,256]{3,2,1,0:T(8,128)S(1)} %shard_map.166.bias1_ref) | copy-start | bytes 3538948
  22.6 0.7 copy-start.2
  23.2 0.7 copy-start.4
  25.6 15.3 %collective-permute-start.4 = (bf16[2,12,3,8,128]{4,3,2,1,0:T(8,128)(2,1)}, bf16[2,12,3,8,128]{4,3,2,1,0:T(8,128)(2,1)S(1)}, u32[]{:S(2)}, u32[]{:S(2)}) collective-permute-start(bf16[2,12,3,8,128]{4,3,2,1,0:T(8,128)(2,1)} %get-tuple-element.15), channel_id=1, source_target_pairs={{120,0},{121,1},{122,2},{123,3},{124,4},{125,5},{126,6},{127,7},{0... | collective-permute-start | bytes 442376 | tf_op jit(solution)/shard_map/ppermute | solution.py:369
  25.6 15.3 %collective-permute-start.5 = (bf16[2,12,3,8,128]{4,3,2,1,0:T(8,128)(2,1)}, bf16[2,12,3,8,128]{4,3,2,1,0:T(8,128)(2,1)S(1)}, u32[]{:S(2)}, u32[]{:S(2)}) collective-permute-start(bf16[2,12,3,8,128]{4,3,2,1,0:T(8,128)(2,1)} %get-tuple-element.16), channel_id=1, source_target_pairs={{8,0},{9,1},{10,2},{11,3},{12,4},{13,5},{14,6},{15,7},{16,8},{17,9... | collective-permute-start | bytes 442376 | tf_op jit(solution)/shard_map/ppermute | solution.py:369
  32.3 0.9 %copy-start.14 = (bf16[2,3,144,128]{3,2,1,0:T(8,128)(2,1)S(1)}, bf16[2,3,144,128]{3,2,1,0:T(8,128)(2,1)}, u32[]{:S(2)}) copy-start(bf16[2,3,144,128]{3,2,1,0:T(8,128)(2,1)} %constant.29.clone.lanes_ref) | copy-start | bytes 663556
  33.2 0.9 %copy-start.16 = (bf16[3,48,144]{2,1,0:T(8,128)(2,1)S(1)}, bf16[3,48,144]{2,1,0:T(8,128)(2,1)}, u32[]{:S(2)}) copy-start(bf16[3,48,144]{2,1,0:T(8,128)(2,1)} %constant.28.clone.keys_ref) | copy-start | bytes 124420
  34.1 6.8 %copy-start.1 = (bf16[8,6,72,192]{3,2,1,0:T(8,128)(2,1)S(1)}, bf16[8,6,72,192]{3,2,1,0:T(8,128)(2,1)}, u32[]{:S(2)}) copy-start(bf16[8,6,72,192]{3,2,1,0:T(8,128)(2,1)} %own_ref.1) | copy-start | bytes 3981316
  34.1 6.8 %copy-start.3 = (bf16[12,6,8,128]{3,2,1,0:T(8,128)(2,1)S(1)}, bf16[12,6,8,128]{3,2,1,0:T(8,128)(2,1)}, u32[]{:S(2)}) copy-start(bf16[12,6,8,128]{3,2,1,0:T(8,128)(2,1)} %copy-done.2) | copy-start | bytes 442372
  34.1 6.8 %copy-start.5 = (bf16[12,6,8,128]{3,2,1,0:T(8,128)(2,1)S(1)}, bf16[12,6,8,128]{3,2,1,0:T(8,128)(2,1)}, u32[]{:S(2)}) copy-start(bf16[12,6,8,128]{3,2,1,0:T(8,128)(2,1)} %copy-done.4) | copy-start | bytes 442372
  34.1 6.8 %copy-start.6 = (bf16[192,768]{1,0:T(8,128)(2,1)S(1)}, bf16[192,768]{1,0:T(8,128)(2,1)}, u32[]{:S(2)}) copy-start(bf16[192,768]{1,0:T(8,128)(2,1)} %wup_ref.1) | copy-start | bytes 884740
  34.1 6.9 %copy-start.7 = (bf16[192,576]{1,0:T(8,128)(2,1)S(1)}, bf16[192,576]{1,0:T(8,128)(2,1)}, u32[]{:S(2)}) copy-start(bf16[192,576]{1,0:T(8,128)(2,1)} %wqkv_ref.1) | copy-start | bytes 663556
  34.1 6.9 %copy-start.9 = (bf16[192,192]{1,0:T(8,128)(2,1)S(1)}, bf16[192,192]{1,0:T(8,128)(2,1)}, u32[]{:S(2)}) copy-start(bf16[192,192]{1,0:T(8,128)(2,1)} %wproj_ref.1) | copy-start | bytes 221188
  34.1 6.8 %copy-start.10 = (f32[192]{0:T(256)S(1)}, f32[192]{0:T(256)}, u32[]{:S(2)}) copy-start(f32[192]{0:T(256)} %param.20) | copy-start | bytes 2308
  34.1 6.8 %copy-start.11 = (f32[192]{0:T(256)S(1)}, f32[192]{0:T(256)}, u32[]{:S(2)}) copy-start(f32[192]{0:T(256)} %param.23) | copy-start | bytes 2308
  34.2 6.8 %copy-start.12 = (bf16[504,432]{1,0:T(8,128)(2,1)S(1)}, bf16[504,432]{1,0:T(8,128)(2,1)}, u32[]{:S(2)}) copy-start(bf16[504,432]{1,0:T(8,128)(2,1)} %constant.30.clone.perm_ref) | copy-start | bytes 1306372
  34.2 6.8 %copy-start.13 = (bf16[432,480]{1,0:T(8,128)(2,1)S(1)}, bf16[432,480]{1,0:T(8,128)(2,1)}, u32[]{:S(2)}) copy-start(bf16[432,480]{1,0:T(8,128)(2,1)} %constant.33.clone.back_ref) | copy-start | bytes 1244164
  34.2 6.8 %copy-start.18 = (bf16[72,48]{1,0:T(8,128)(2,1)S(1)}, bf16[72,48]{1,0:T(8,128)(2,1)}, u32[]{:S(2)}) copy-start(bf16[72,48]{1,0:T(8,128)(2,1)} %constant.32.clone.right_ref) | copy-start | bytes 20740
  34.2 6.8 %copy-start.19 = (bf16[72,48]{1,0:T(8,128)(2,1)S(1)}, bf16[72,48]{1,0:T(8,128)(2,1)}, u32[]{:S(2)}) copy-start(bf16[72,48]{1,0:T(8,128)(2,1)} %constant.31.clone.left_ref) | copy-start | bytes 20740
  34.2 6.8 %copy-start.21 = (f32[4,2,144,256]{3,2,1,0:T(8,128)S(1)}, f32[4,2,144,256]{3,2,1,0:T(8,128)}, u32[]{:S(2)}) copy-start(f32[4,2,144,256]{3,2,1,0:T(8,128)} %copy-done.20) | copy-start | bytes 3538948

commit v3 on v2

v3 whole, which is shorter than its diff:
```python
import jax
import jax.numpy as jnp
import numpy as np
from jax import lax
from jax.experimental import pallas as pl
from jax.experimental.pallas import tpu as pltpu
from jax.sharding import PartitionSpec as P

HEADS = 6
HD = 32
C = 192
FFH = 768
ZW = 4
COLS = 72
UNITS = 12
WINS = 7
SLOT = 40
ROWS = 1008
NEG = -1e30
LOG2E = 1.4426950408889634
EPS = 1e-05
F32 = jnp.float32
BF16 = jnp.bfloat16
GELU = (0.7978697125591424, 0.036392285416293954, -8.782600959854813e-05, -3.66935623623972e-05, 1.4250130824069052e-06)


def head_row(h):
    return h * SLOT + (8 if h >= 3 else 0)


def unit_place(c):
    return (c + 1) // 2, (c + 1) % 2


def gather_maps():
    perm = np.zeros((504, 432), np.float32)
    left = np.zeros((72, 48), np.float32)
    right = np.zeros((72, 48), np.float32)
    back = np.zeros((440, 480), np.float32)
    for c in range(-1, 13):
        m, half = unit_place(c)
        for r in range(6):
            for j in range(6):
                row = 72 * m + 36 * half + r * 6 + j
                if c == -1:
                    left[row, r * 8 + 2 + j] = 1
                elif c == 12:
                    right[row - 432, r * 8 + j] = 1
                else:
                    perm[row, r * COLS + 6 * c + j] = 1
                    back[r * COLS + 6 * c + j, c * SLOT + 4 * half + r * 6 + j] = 1
    return [x.astype(jnp.bfloat16) for x in (perm, left, right, back)]


def place_of(rest, half, upper):
    dz = (rest >= 18).astype(jnp.int32)
    rest = rest - 18 * dz
    di = (rest >= 6).astype(jnp.int32) + (rest >= 12).astype(jnp.int32)
    return (6 * dz + 3 * upper + di) * 12 + 6 * half + rest - 6 * di


def one_hot(mask):
    return jnp.where(mask, 1.0, 0.0).astype(BF16)


def key_map(latw, third):
    rest = lax.broadcasted_iota(jnp.int32, (48, 144), 0) + 48 * third
    halo = (rest >= 72).astype(jnp.int32)
    rest = rest - 72 * halo
    half = (rest >= 36).astype(jnp.int32)
    upper = halo if latw else 1 - halo
    return one_hot(lax.broadcasted_iota(jnp.int32, (48, 144), 1) == place_of(rest - 36 * half, half, upper))


def lane_map(latw, half, third):
    slot = lax.broadcasted_iota(jnp.int32, (144, 128), 1) - (SLOT * third + 4 * half)
    place = place_of(slot, half, 1 - latw)
    mine = (slot >= 0) & (slot < 36) & (lax.broadcasted_iota(jnp.int32, (144, 128), 0) == place)
    return one_hot(mine)


def nt(a, b):
    return lax.dot_general(a, b, (((1,), (1,)), ((), ())), preferred_element_type=F32)


def tn(a, b):
    return lax.dot_general(a, b, (((0,), (0,)), ((), ())), preferred_element_type=F32)


def nn(a, b):
    return jnp.dot(a, b, preferred_element_type=F32)


POS = 3312
CH = 13


def bias_kernel(cut_ref, table1_ref, table0_ref, index_ref, out_ref, ts, lo_s, hi_s, g_s):
    for latw, table_ref in enumerate((table0_ref, table1_ref)):
        for ch in range(CH):
            width = min(256, POS - 256 * ch)
            rows = jnp.concatenate([table_ref[0, h, :, 256 * ch : 256 * ch + width] for h in range(HEADS)], axis=0)
            if width < 256:
                rows = jnp.concatenate([rows, jnp.zeros((24, 256 - width), F32)], axis=1)
            rows = rows * LOG2E
            top = rows.astype(BF16).astype(F32)
            ts[latw, 24 * ch : 24 * ch + 24] = top
            ts[latw, 24 * (CH + ch) : 24 * (CH + ch) + 24] = rows - top
    index = index_ref[...]
    index_lo = (index & 255).astype(F32).astype(BF16)
    index_hi = (index >> 8).astype(F32).astype(BF16)
    for latw in range(2):
        maps = [[lane_map(latw, half, third) for third in range(3)] for half in range(2)]
        keys = [key_map(latw, third) for third in range(3)]
        for part, dst in ((index_lo, lo_s), (index_hi, hi_s)):
            rows = [nt(keys[third], part).astype(BF16) for third in range(3)]
            for half in range(2):
                total = nn(rows[0], maps[half][0])
                for third in range(1, 3):
                    total = total + nn(rows[third], maps[half][third])
                dst[latw, 48 * half : 48 * half + 48] = total
    spread = lax.broadcasted_iota(jnp.int32, (256, 128), 0).astype(F32).astype(BF16)
    for latw in range(2):
        both = ts[latw].astype(BF16)

        def step(i, _):
            los = [lo_s[latw, pl.ds(i + 48 * half, 1), :].astype(BF16) for half in range(2)]
            his = jnp.concatenate([hi_s[latw, pl.ds(i + 48 * half, 1), :] for half in range(2)], axis=1)
            hot = jnp.concatenate([jnp.where(spread == v, BF16(1), BF16(0)) for v in los], axis=1)
            vals = nn(both, hot)
            vals = vals[: 24 * CH] + vals[24 * CH :]
            his = jnp.broadcast_to(his, (24, 256))
            acc = vals[0:24]
            for ch in range(1, CH):
                acc = jnp.where(his == float(ch), vals[24 * ch : 24 * ch + 24], acc)
            g_s[latw, i] = acc
            return 0

        lax.fori_loop(0, 48, step, 0, unroll=True)
    lane = lax.broadcasted_iota(jnp.int32, (8, 128), 1)
    for latw in range(2):
        cut = cut_ref[latw] == 1
        for z in range(ZW):
            for half in range(2):
                for tile in range(2):
                    for k8 in range(6):
                        three = [
                            g_s[latw, 8 * k8 : 8 * k8 + 8, (3 * tile + h) * ZW + z, 128 * half : 128 * half + 128]
                            for h in range(3)
                        ]
                        for third in range(3):
                            moved = [
                                three[h] if h == third else pltpu.roll(three[h], (SLOT * (h - third)) % 128, 1)
                                for h in range(3)
                            ]
                            got = jnp.where(lane < SLOT, moved[0], jnp.where(lane < 2 * SLOT, moved[1], moved[2]))
                            row = 48 * third + 8 * k8
                            if row >= 72:
                                got = jnp.where(cut, NEG, got)
                            out_ref[latw, z, half, row : row + 8, 128 * tile : 128 * tile + 128] = got


def make_bias(cut, table1, table0, index_table):
    return pl.pallas_call(
        bias_kernel,
        out_shape=jax.ShapeDtypeStruct((2, ZW, 2, 144, 256), F32),
        in_specs=[pl.BlockSpec(memory_space=pltpu.SMEM)] + [pl.BlockSpec(memory_space=pltpu.VMEM)] * 3,
        out_specs=pl.BlockSpec(memory_space=pltpu.VMEM),
        scratch_shapes=[
            pltpu.VMEM((2, 48 * CH, 256), F32),
            pltpu.VMEM((2, 96, 128), F32),
            pltpu.VMEM((2, 96, 128), F32),
            pltpu.VMEM((2, 48, 24, 256), F32),
        ],
        compiler_params=pltpu.CompilerParams(vmem_limit_bytes=16 * 2**20),
        cost_estimate=pl.CostEstimate(flops=14 * 10**9, bytes_accessed=2 * 10**6, transcendentals=0),
    )(cut, table1, table0, index_table)


def packed_shape(levels, rows, cols):
    return jax.ShapeDtypeStruct((3 * levels // 2, rows, cols, 128), BF16)


def pack(dst, x):
    levels = x.shape[0]
    dst[:levels] = x[..., :128]
    for i in range(levels // 2):
        dst[levels + i] = jnp.concatenate([x[2 * i, ..., 128:], x[2 * i + 1, ..., 128:]], axis=-1)


def unpack(src, levels, z):
    low = src[pl.ds(2 * z, 2)].astype(F32)
    high = src[pl.ds(levels + z, 1)].astype(F32)
    rows = low.shape[1] * low.shape[2]
    low = low.reshape(2, rows, 128)
    high = high.reshape(rows, 128)
    parts = [jnp.concatenate([low[dz], high[:, 64 * dz : 64 * dz + 64]], axis=1) for dz in range(2)]
    return jnp.concatenate(parts, axis=0).astype(BF16)


def pack_kernel(x_ref, up, dn, er, el):
    pack(up, x_ref[:, 3:6])
    pack(dn, x_ref[:, 0:3])
    pack(er, x_ref[:, :, COLS - 8 :])
    pack(el, x_ref[:, :, :8])


def make_packs(tokens):
    vmem = pl.BlockSpec(memory_space=pltpu.VMEM)
    shapes = [packed_shape(8, 3, COLS)] * 2 + [packed_shape(8, 6, 8)] * 2
    return pl.pallas_call(
        pack_kernel,
        out_shape=shapes,
        in_specs=[vmem],
        out_specs=[vmem] * len(shapes),
        compiler_params=pltpu.CompilerParams(vmem_limit_bytes=16 * 2**20),
    )(tokens)


def rim_kernel(l_ref, r_ref, up, dn):
    for side, ref in enumerate((l_ref, r_ref)):
        up[side] = ref[:, 3:6]
        dn[side] = ref[:, 0:3]


def make_rims(left, right):
    vmem = pl.BlockSpec(memory_space=pltpu.VMEM)
    shape = jax.ShapeDtypeStruct((2, 12, 3, 8, 128), BF16)
    return pl.pallas_call(rim_kernel, out_shape=[shape] * 2, in_specs=[vmem] * 2, out_specs=[vmem] * 2,
                          compiler_params=pltpu.CompilerParams(vmem_limit_bytes=8 * 2**20))(left, right)


def block_kernel(own_ref, prev_ref, next_ref, l_ref, r_ref, cp_ref, cn_ref, bias_ref,
                 ga_ref, wqkv_ref, wproj_ref, gm_ref, wup_ref, wdown_ref,
                 perm_ref, left_ref, right_ref, back_ref, out_ref,
                 xs, ns, qs, kvs, os_, rs, ob, ss, ps, sems):
    def flat(v):
        return v.astype(F32).reshape(-1, C).astype(BF16)

    ones = jnp.ones((C, 128), BF16)
    gain = ga_ref[...]
    lane = lax.broadcasted_iota(jnp.int32, (SLOT, C), 1) // HD
    pad = jnp.zeros((8, C), F32)

    def both(v):
        return jnp.concatenate([v, v[:, : C - 128]], axis=1)

    halves = [(latw, c) for latw in range(2) for c in range(UNITS)]

    def gather(z, latw):
        levels = pl.ds(2 * z, 2)
        row = 3 * latw
        own = flat(own_ref[levels, row : row + 3])
        halo = unpack(next_ref if latw else prev_ref, 8, z)
        perm = perm_ref[...]
        own_edges = [unpack(e.at[:, row : row + 3], 8, z) for e in (l_ref, r_ref)]
        halo_edges = [unpack((cn_ref if latw else cp_ref).at[side], 8, z) for side in range(2)]
        for base, block, edges in ((0, own, own_edges), (72, halo, halo_edges)):
            got = nn(perm, block)
            edge_l = nn(left_ref[...], edges[0])
            edge_r = nn(right_ref[...], edges[1])
            for m in range(WINS):
                piece = got[72 * m : 72 * m + 72]
                if m == 0:
                    piece = piece + edge_l
                if m == WINS - 1:
                    piece = piece + edge_r
                first = ROWS * latw + 144 * m + base
                xs[first : first + 72] = piece

    def first_norm(r0):
        x = xs[r0 : r0 + 144]
        mean = both(nn(x.astype(BF16), ones) * (1.0 / C))
        cen = x - mean
        var = nn((cen * cen).astype(BF16), ones) * (1.0 / C)
        inv = both(lax.rsqrt(var + EPS))
        ns[r0 : r0 + 144] = (cen * inv * gain).astype(BF16)

    def scores(z, latw, c):
        m, half = unit_place(c)
        r0 = ROWS * latw + 144 * m
        q = qs[r0 + 32 * half : r0 + 32 * half + SLOT]
        rows = []
        for h in range(HEADS):
            rows.append(jnp.where(lane == h, q, 0.0))
            if h in (2, 5):
                rows.append(pad)
        qm = jnp.concatenate(rows, axis=0).astype(BF16)
        return nt(kvs[r0 : r0 + 144, :C], qm) + bias_ref[latw, z, half]

    def soft(s):
        e = jnp.exp2(s - jnp.max(s, axis=0, keepdims=True))
        return (e * (1.0 / jnp.sum(e, axis=0, keepdims=True))).astype(BF16)

    def attend(latw, c, p):
        m, half = unit_place(c)
        r0 = ROWS * latw + 144 * m
        o = tn(p, kvs[r0 : r0 + 144, C:])
        out = o[0:SLOT]
        for h in range(1, HEADS):
            out = jnp.where(lane == h, o[head_row(h) : head_row(h) + SLOT], out)
        to = SLOT * (UNITS * latw + c)
        os_[to : to + SLOT] = out
        rs[to : to + SLOT] = xs[r0 + 32 * half : r0 + 32 * half + SLOT]

    def level_pair(z):
        for latw in range(2):
            gather(z, latw)
        for r0 in range(0, 2 * ROWS, 144):
            first_norm(r0)
        packed = nn(ns[...], wqkv_ref[...])
        qs[...] = packed[:, :C] * (HD ** -0.5 * LOG2E)
        kvs[...] = packed[:, C:].astype(BF16)
        for n, (latw, c) in enumerate(halves):
            ss[n] = scores(z, latw, c)
        for n in range(2 * UNITS):
            ps[n] = soft(ss[n])
        for n, (latw, c) in enumerate(halves):
            attend(latw, c, ps[n])
        resid = rs[...] + nn(os_[...].astype(BF16), wproj_ref[...])
        mean = jnp.mean(resid, axis=1, keepdims=True)
        cen = resid - mean
        var = nn((cen * cen).astype(BF16), ones) * (1.0 / C)
        normed = (cen * both(lax.rsqrt(var + EPS)) * gm_ref[...]).astype(BF16)
        u = nn(normed, wup_ref[...])
        w = u * u
        poly = w * GELU[-1] + GELU[-2]
        for coef in GELU[-3::-1]:
            poly = poly * w + coef
        hidden = (u + u * jnp.tanh(u * poly)).astype(BF16)
        out = (resid + 0.5 * nt(hidden, wdown_ref[...])).astype(BF16)
        for latw in range(2):
            got = nn(back_ref[:432], out[SLOT * UNITS * latw : SLOT * UNITS * (latw + 1)])
            ob[z, :, 3 * latw : 3 * latw + 3] = got.reshape(2, 3, COLS, C).astype(BF16)

    def leave(z):
        return pltpu.make_async_copy(ob.at[z], out_ref.at[pl.ds(2 * z, 2)], sems.at[z])

    def step(z, _):
        level_pair(z)
        leave(z).start()
        return 0

    lax.fori_loop(0, ZW, step, 0)
    for z in range(ZW):
        leave(z).wait()


def run_block(tokens, halos, edges, bias, weights, maps):
    vmem = pl.BlockSpec(memory_space=pltpu.VMEM)
    operands = (tokens, *halos, *edges, bias, *weights, *maps)
    return pl.pallas_call(
        block_kernel,
        out_shape=jax.ShapeDtypeStruct(tokens.shape, BF16),
        in_specs=[vmem] * len(operands),
        out_specs=pl.BlockSpec(memory_space=pl.ANY),
        scratch_shapes=[
            pltpu.VMEM((2 * ROWS, C), F32),
            pltpu.VMEM((2 * ROWS, C), BF16),
            pltpu.VMEM((2 * ROWS, C), F32),
            pltpu.VMEM((2 * ROWS, 2 * C), BF16),
            pltpu.VMEM((2 * SLOT * UNITS, C), F32),
            pltpu.VMEM((2 * SLOT * UNITS, C), F32),
            pltpu.VMEM((ZW, 2, 6, COLS, C), BF16),
            pltpu.VMEM((2 * UNITS, 144, 256), F32),
            pltpu.VMEM((2 * UNITS, 144, 256), BF16),
            pltpu.SemaphoreType.DMA((ZW,)),
        ],
        compiler_params=pltpu.CompilerParams(vmem_limit_bytes=36 * 2**20),
        cost_estimate=pl.CostEstimate(flops=30 * 10**9, bytes_accessed=2 * 10**6, transcendentals=0),
    )(*operands)


def passed_along(block, lat, lon):
    nlat, nlon = lax.axis_size("lat"), lax.axis_size("lon")
    route = [
        (((i - lat) % nlat) * nlon + (j - lon) % nlon, i * nlon + j) for i in range(nlat) for j in range(nlon)
    ]
    return lax.ppermute(block, ("lat", "lon"), route)


def shards(tokens, bias_table, index_table, gain_attn, w_qkv, w_proj, gain_mlp, w_up, w_down):
    place = lax.axis_index("lat")
    last = lax.axis_size("lat") - 1
    up, dn, er, el = make_packs(tokens)
    table = bias_table.transpose(0, 2, 1, 3)
    prev_table = passed_along(table, 1, 0)
    halos = (passed_along(up, 1, 0), passed_along(dn, -1, 0))
    left, right = passed_along(er, 0, 1), passed_along(el, 0, -1)
    rim_up, rim_dn = make_rims(left, right)
    edges = (left, right, passed_along(rim_up, 1, 0), passed_along(rim_dn, -1, 0))
    maps = gather_maps()
    cut = jnp.stack([place == 0, place == last]).astype(jnp.int32)
    bias = make_bias(cut, table, prev_table, index_table)
    weights = (gain_attn.reshape(1, C), w_qkv, w_proj, gain_mlp.reshape(1, C), w_up, w_down.T)
    return run_block(tokens, halos, edges, bias, weights, maps)


def solution(mesh):
    return jax.shard_map(
        shards,
        mesh=mesh,
        in_specs=(
            P(None, "lat", "lon", None),
            P("lat", None, None, None),
            P(),
            P(),
            P(),
            P(),
            P(),
            P(),
            P(),
        ),
        out_specs=P(None, "lat", "lon", None),
        check_vma=False,
    )
```

time: 75.7 us -> 61.7 us (0.82)
  Pallas kernels: 49.5 us -> 40.6 us
  local copies, waits for them, and re-layouts: 10.1 us -> 1.56 us
  waiting for transfers between devices: 0.02 us -> 3.24 us
    unnamed x46 -> x28, local copies, waits for them, and re-layouts: 7.91 us -> 1.56 us
    pallas_call x1, Pallas kernels: 34.1 us -> 28.7 us  [run_block(): pl.pallas_call(block_kernel, out_shape=jax.ShapeDtypeStruct(tokens.shape,...]
    ppermute x7, waiting for transfers between devices: 0.02 us -> 3.24 us  [passed_along(): return lax.ppermute(block, ('lat', 'lon'), route)]
    pallas_call x2 -> x1, Pallas kernels: 13.3 us -> 10.9 us  [make_bias(): pl.pallas_call(bias_kernel, out_shape=jax.ShapeDtypeStruct((2, ZW, 2, 144...]
    reshape x2 -> x0, local copies, waits for them, and re-layouts: 2.22 us -> none  [the longest x1 1.28 us: shards(): passed_along(bias_table.reshape(-1, 128), 1, 0).reshape(bias_table.shape)]
    pallas_call x1, Pallas kernels: 1.75 us -> 0.03 us  [make_rims(): pl.pallas_call(rim_kernel, out_shape=[shape] * 2, in_specs=[vmem] * 2, ou...]
  transfers between devices with their start and end apart: 7 -> 7, of which waited for: 0 -> 1; matrix products, arithmetic and copies ran while one was open for 3% -> 0% of each run, Pallas kernels for 20% -> 19%
where the time goes in v3:
time: 61.7 us; the launch traced here: 61.2 us
  Pallas kernels  40.6 us (66%)
  starting transfers between devices  15.4 us (25%)
  waiting for transfers between devices  3.24 us (5%)
  local copies, waits for them, and re-layouts  1.56 us (3%)
    pallas_call x1, Pallas kernels, run_block(): pl.pallas_call(block_kernel, out_shape=jax.ShapeDtypeStruct(tokens.shape,...  28.7 us
    ppermute x7, starting transfers between devices, passed_along(): return lax.ppermute(block, ('lat', 'lon'), route)  15.4 us
    pallas_call x1, Pallas kernels, make_bias(): pl.pallas_call(bias_kernel, out_shape=jax.ShapeDtypeStruct((2, ZW, 2, 144...  10.9 us
    ppermute x7, waiting for transfers between devices, passed_along(): return lax.ppermute(block, ('lat', 'lon'), route)  3.24 us
    unnamed x28, local copies, waits for them, and re-layouts  1.56 us
  transfers between devices with their start and end apart: 7, of which 1 were waited for; matrix products, arithmetic and copies ran while one was open for 0% of the time, Pallas kernels for 19%

profile of v3, /device:TPU:0, one launch (start us, length us, event | category | flops | bytes accessed | tf_op | source)
XLA Modules:
  0.0 61.2 jit_solution(1236487052770882863)
XLA Ops:
  0.0 0.0 collective-permute-start.6
  0.0 0.0 copy-start
  0.0 1.5 %copy-done = bf16[8,6,72,192]{3,2,1,0:T(8,128)(2,1)S(1)} copy-done((bf16[8,6,72,192]{3,2,1,0:T(8,128)(2,1)S(1)}, bf16[8,6,72,192]{3,2,1,0:T(8,128)(2,1)}, u32[]{:S(2)}) %copy-start) | copy-done | bytes 1327128
  1.5 0.0 copy-start.2
  1.5 0.0 copy-start.6
  1.5 1.0 %shard_map.127 = (bf16[12,3,72,128]{3,2,1,0:T(8,128)(2,1)S(1)}, bf16[12,3,72,128]{3,2,1,0:T(8,128)(2,1)S(1)}, bf16[12,6,8,128]{3,2,1,0:T(8,128)(2,1)}, bf16[12,6,8,128]{3,2,1,0:T(8,128)(2,1)}) custom-call(bf16[8,6,72,192]{3,2,1,0:T(8,128)(2,1)S(1)} %copy-done), custom_call_target="tpu_custom_call" | custom-call | tf_op jit(solution)/shard_map/pallas_call | solution.py:211
  2.5 1.6 %collective-permute-start.2 = (bf16[12,6,8,128]{3,2,1,0:T(8,128)(2,1)}, bf16[12,6,8,128]{3,2,1,0:T(8,128)(2,1)S(1)}, u32[]{:S(2)}, u32[]{:S(2)}) collective-permute-start(bf16[12,6,8,128]{3,2,1,0:T(8,128)(2,1)} %get-tuple-element.13), channel_id=1, source_target_pairs={{7,0},{0,1},{1,2},{2,3},{3,4},{4,5},{5,6},{6,7},{15,8},{8,9},{9,10... | collective-permute-start | bytes 442376 | tf_op jit(solution)/shard_map/ppermute | solution.py:379
  4.1 2.6 %collective-permute-start.3 = (bf16[12,6,8,128]{3,2,1,0:T(8,128)(2,1)}, bf16[12,6,8,128]{3,2,1,0:T(8,128)(2,1)S(1)}, u32[]{:S(2)}, u32[]{:S(2)}) collective-permute-start(bf16[12,6,8,128]{3,2,1,0:T(8,128)(2,1)} %get-tuple-element.14), channel_id=1, source_target_pairs={{1,0},{2,1},{3,2},{4,3},{5,4},{6,5},{7,6},{0,7},{9,8},{10,9},{11,1... | collective-permute-start | bytes 442376 | tf_op jit(solution)/shard_map/ppermute | solution.py:379
  6.7 2.8 %collective-permute-start = (bf16[12,3,72,128]{3,2,1,0:T(8,128)(2,1)S(1)}, bf16[12,3,72,128]{3,2,1,0:T(8,128)(2,1)S(1)}, u32[]{:S(2)}, u32[]{:S(2)}) collective-permute-start(bf16[12,3,72,128]{3,2,1,0:T(8,128)(2,1)S(1)} %get-tuple-element.11), channel_id=1, source_target_pairs={{120,0},{121,1},{122,2},{123,3},{124,4},{125,5},{126,6},{127,7},{0... | collective-permute-start | bytes 1990664 | tf_op jit(solution)/shard_map/ppermute | solution.py:379
  9.5 2.8 %collective-permute-start.1 = (bf16[12,3,72,128]{3,2,1,0:T(8,128)(2,1)S(1)}, bf16[12,3,72,128]{3,2,1,0:T(8,128)(2,1)S(1)}, u32[]{:S(2)}, u32[]{:S(2)}) collective-permute-start(bf16[12,3,72,128]{3,2,1,0:T(8,128)(2,1)S(1)} %get-tuple-element.12), channel_id=1, source_target_pairs={{8,0},{9,1},{10,2},{11,3},{12,4},{13,5},{14,6},{15,7},{16,8},{17,9... | collective-permute-start | bytes 1990664 | tf_op jit(solution)/shard_map/ppermute | solution.py:379
  12.3 0.1 add_convert_fusion.cut_ref
  12.4 0.0 collective-permute-done.2.l_ref
  12.4 0.0 collective-permute-done.3.r_ref
  12.4 0.1 collective-permute-start.4
  12.5 0.0 copy-start.1
  12.5 0.0 copy-start.3
  12.5 0.0 copy-start.4
  12.5 0.0 copy-start.5
  12.5 0.0 copy-start.7
  12.5 0.0 copy-start.8
  12.6 0.0 copy-start.9
  12.6 0.0 copy-start.10
  12.6 0.0 copy-start.11
  12.6 0.0 copy-start.12
  12.6 0.0 copy-start.13
  12.6 5.6 %collective-permute-start.5 = (bf16[2,12,3,8,128]{4,3,2,1,0:T(8,128)(2,1)S(1)}, bf16[2,12,3,8,128]{4,3,2,1,0:T(8,128)(2,1)S(1)}, u32[]{:S(2)}, u32[]{:S(2)}) collective-permute-start(bf16[2,12,3,8,128]{4,3,2,1,0:T(8,128)(2,1)S(1)} %get-tuple-element.16), channel_id=1, source_target_pairs={{8,0},{9,1},{10,2},{11,3},{12,4},{13,5},{14,6},{15,7},{16,8},{17,9... | collective-permute-start | bytes 442376 | tf_op jit(solution)/shard_map/ppermute | solution.py:379
  18.2 0.0 collective-permute-done.6.table0_ref
  18.2 0.0 copy-done.2
  18.2 0.0 copy-done.6
  18.2 10.9 %shard_map.129.bias_ref = f32[2,4,2,144,256]{4,3,2,1,0:T(8,128)S(1)} custom-call(s32[2]{0:T(128)S(1)} %add_convert_fusion.cut_ref, f32[1,6,4,3312]{3,2,1,0:T(4,128)S(1)} %bitcast.7, f32[1,6,4,3312]{3,2,1,0:T(4,128)} %collective-permute-done.6.table0_ref, s32[144,144]{1,0:T(8,128)S(1)} %copy-done.6), custom_call_target="tpu_custom_call" | custom-call | flops 14000000000 | bytes 2000000 | tf_op jit(solution)/shard_map/pallas_call | solution.py:164
  29.1 3.2 %collective-permute-done.4.cp_ref = bf16[2,12,3,8,128]{4,3,2,1,0:T(8,128)(2,1)S(1)} collective-permute-done((bf16[2,12,3,8,128]{4,3,2,1,0:T(8,128)(2,1)S(1)}, bf16[2,12,3,8,128]{4,3,2,1,0:T(8,128)(2,1)S(1)}, u32[]{:S(2)}, u32[]{:S(2)}) %collective-permute-start.4) | collective-permute-done | bytes 147488 | tf_op jit(solution)/shard_map/ppermute | solution.py:379
  32.3 0.0 collective-permute-done.5.cn_ref
  32.3 0.0 collective-permute-done.prev_ref
  32.3 0.0 collective-permute-done.1.next_ref
  32.3 0.0 copy-done.1
  32.3 0.0 copy-done.3
  32.3 0.0 copy-done.4
  32.3 0.0 copy-done.5
  32.3 0.0 copy-done.7
  32.3 0.0 copy-done.8
  32.4 0.0 copy-done.9
  32.4 0.0 copy-done.10
  32.4 0.0 copy-done.11
  32.4 0.0 copy-done.12
  32.4 0.0 copy-done.13
  32.4 28.7 %shard_map.130 = bf16[8,6,72,192]{3,2,1,0:T(8,128)(2,1)} custom-call(bf16[8,6,72,192]{3,2,1,0:T(8,128)(2,1)S(1)} %copy-done.1, bf16[12,3,72,128]{3,2,1,0:T(8,128)(2,1)S(1)} %collective-permute-done.prev_ref, bf16[12,3,72,128]{3,2,1,0:T(8,128)(2,1)S(1)} %collective-permute-done.1.next_ref, bf16[12,6,8,128]{3,2,1,0:T(8,128)(2,1)S(1)} %collective-permute-done.2.l_ref, ...), custom_call_target="tpu_custom_call" | custom-call | flops 30000001024 | bytes 2000000 | tf_op jit(solution)/shard_map/pallas_call | solution.py:352
  (1 shorter events, 0.0 us)
Async XLA Ops:
  0.0 18.2 %collective-permute-start.6 = (f32[1,6,4,3312]{3,2,1,0:T(4,128)}, f32[1,6,4,3312]{3,2,1,0:T(4,128)}, u32[]{:S(2)}, u32[]{:S(2)}) collective-permute-start(f32[1,6,4,3312]{3,2,1,0:T(4,128)} %bitcast.6), channel_id=1, source_target_pairs={{120,0},{121,1},{122,2},{123,3},{124,4},{125,5},{126,6},{127,7},{0... | collective-permute-start | bytes 953864 | tf_op jit(solution)/shard_map/ppermute | solution.py:379
  0.0 1.5 %copy-start = (bf16[8,6,72,192]{3,2,1,0:T(8,128)(2,1)S(1)}, bf16[8,6,72,192]{3,2,1,0:T(8,128)(2,1)}, u32[]{:S(2)}) copy-start(bf16[8,6,72,192]{3,2,1,0:T(8,128)(2,1)} %own_ref.1) | copy-start | bytes 3981316
  1.5 16.7 %copy-start.2 = (f32[1,4,6,3312]{3,1,2,0:T(4,128)S(1)}, f32[1,4,6,3312]{3,1,2,0:T(4,128)}, u32[]{:S(2)}) copy-start(f32[1,4,6,3312]{3,1,2,0:T(4,128)} %param.14) | copy-start | bytes 953860
  1.5 16.7 %copy-start.6 = (s32[144,144]{1,0:T(8,128)S(1)}, s32[144,144]{1,0:T(8,128)}, u32[]{:S(2)}) copy-start(s32[144,144]{1,0:T(8,128)} %index_ref.1) | copy-start | bytes 248836
  2.5 9.8 %collective-permute-start.2 = (bf16[12,6,8,128]{3,2,1,0:T(8,128)(2,1)}, bf16[12,6,8,128]{3,2,1,0:T(8,128)(2,1)S(1)}, u32[]{:S(2)}, u32[]{:S(2)}) collective-permute-start(bf16[12,6,8,128]{3,2,1,0:T(8,128)(2,1)} %get-tuple-element.13), channel_id=1, source_target_pairs={{7,0},{0,1},{1,2},{2,3},{3,4},{4,5},{5,6},{6,7},{15,8},{8,9},{9,10... | collective-permute-start | bytes 442376 | tf_op jit(solution)/shard_map/ppermute | solution.py:379
  4.1 8.3 %collective-permute-start.3 = (bf16[12,6,8,128]{3,2,1,0:T(8,128)(2,1)}, bf16[12,6,8,128]{3,2,1,0:T(8,128)(2,1)S(1)}, u32[]{:S(2)}, u32[]{:S(2)}) collective-permute-start(bf16[12,6,8,128]{3,2,1,0:T(8,128)(2,1)} %get-tuple-element.14), channel_id=1, source_target_pairs={{1,0},{2,1},{3,2},{4,3},{5,4},{6,5},{7,6},{0,7},{9,8},{10,9},{11,1... | collective-permute-start | bytes 442376 | tf_op jit(solution)/shard_map/ppermute | solution.py:379
  6.7 25.6 %collective-permute-start = (bf16[12,3,72,128]{3,2,1,0:T(8,128)(2,1)S(1)}, bf16[12,3,72,128]{3,2,1,0:T(8,128)(2,1)S(1)}, u32[]{:S(2)}, u32[]{:S(2)}) collective-permute-start(bf16[12,3,72,128]{3,2,1,0:T(8,128)(2,1)S(1)} %get-tuple-element.11), channel_id=1, source_target_pairs={{120,0},{121,1},{122,2},{123,3},{124,4},{125,5},{126,6},{127,7},{0... | collective-permute-start | bytes 1990664 | tf_op jit(solution)/shard_map/ppermute | solution.py:379
  9.5 22.8 %collective-permute-start.1 = (bf16[12,3,72,128]{3,2,1,0:T(8,128)(2,1)S(1)}, bf16[12,3,72,128]{3,2,1,0:T(8,128)(2,1)S(1)}, u32[]{:S(2)}, u32[]{:S(2)}) collective-permute-start(bf16[12,3,72,128]{3,2,1,0:T(8,128)(2,1)S(1)} %get-tuple-element.12), channel_id=1, source_target_pairs={{8,0},{9,1},{10,2},{11,3},{12,4},{13,5},{14,6},{15,7},{16,8},{17,9... | collective-permute-start | bytes 1990664 | tf_op jit(solution)/shard_map/ppermute | solution.py:379
  12.4 19.9 %collective-permute-start.4 = (bf16[2,12,3,8,128]{4,3,2,1,0:T(8,128)(2,1)S(1)}, bf16[2,12,3,8,128]{4,3,2,1,0:T(8,128)(2,1)S(1)}, u32[]{:S(2)}, u32[]{:S(2)}) collective-permute-start(bf16[2,12,3,8,128]{4,3,2,1,0:T(8,128)(2,1)S(1)} %get-tuple-element.15), channel_id=1, source_target_pairs={{120,0},{121,1},{122,2},{123,3},{124,4},{125,5},{126,6},{127,7},{0... | collective-permute-start | bytes 442376 | tf_op jit(solution)/shard_map/ppermute | solution.py:379
  12.5 19.8 %copy-start.1 = (bf16[8,6,72,192]{3,2,1,0:T(8,128)(2,1)S(1)}, bf16[8,6,72,192]{3,2,1,0:T(8,128)(2,1)}, u32[]{:S(2)}) copy-start(bf16[8,6,72,192]{3,2,1,0:T(8,128)(2,1)} %own_ref.1) | copy-start | bytes 3981316
  12.5 19.8 %copy-start.3 = (bf16[192,768]{1,0:T(8,128)(2,1)S(1)}, bf16[192,768]{1,0:T(8,128)(2,1)}, u32[]{:S(2)}) copy-start(bf16[192,768]{1,0:T(8,128)(2,1)} %wup_ref.1) | copy-start | bytes 884740
  12.5 19.8 %copy-start.4 = (bf16[768,192]{0,1:T(8,128)(2,1)S(1)}, bf16[768,192]{0,1:T(8,128)(2,1)}, u32[]{:S(2)}) copy-start(bf16[768,192]{0,1:T(8,128)(2,1)} %param.21) | copy-start | bytes 884740
  12.5 19.8 %copy-start.5 = (bf16[192,576]{1,0:T(8,128)(2,1)S(1)}, bf16[192,576]{1,0:T(8,128)(2,1)}, u32[]{:S(2)}) copy-start(bf16[192,576]{1,0:T(8,128)(2,1)} %wqkv_ref.1) | copy-start | bytes 663556
  12.5 19.8 %copy-start.7 = (bf16[192,192]{1,0:T(8,128)(2,1)S(1)}, bf16[192,192]{1,0:T(8,128)(2,1)}, u32[]{:S(2)}) copy-start(bf16[192,192]{1,0:T(8,128)(2,1)} %wproj_ref.1) | copy-start | bytes 221188
  12.5 19.8 %copy-start.8 = (f32[192]{0:T(256)S(1)}, f32[192]{0:T(256)}, u32[]{:S(2)}) copy-start(f32[192]{0:T(256)} %param.16) | copy-start | bytes 2308
  12.6 19.8 %copy-start.9 = (f32[192]{0:T(256)S(1)}, f32[192]{0:T(256)}, u32[]{:S(2)}) copy-start(f32[192]{0:T(256)} %param.19) | copy-start | bytes 2308
  12.6 19.8 %copy-start.10 = (bf16[504,432]{1,0:T(8,128)(2,1)S(1)}, bf16[504,432]{1,0:T(8,128)(2,1)}, u32[]{:S(2)}) copy-start(bf16[504,432]{1,0:T(8,128)(2,1)} %constant.18.clone.perm_ref) | copy-start | bytes 1306372
  12.6 19.8 %copy-start.11 = (bf16[440,480]{1,0:T(8,128)(2,1)S(1)}, bf16[440,480]{1,0:T(8,128)(2,1)}, u32[]{:S(2)}) copy-start(bf16[440,480]{1,0:T(8,128)(2,1)} %constant.21.clone.back_ref) | copy-start | bytes 1267204
  12.6 19.8 %copy-start.12 = (bf16[72,48]{1,0:T(8,128)(2,1)S(1)}, bf16[72,48]{1,0:T(8,128)(2,1)}, u32[]{:S(2)}) copy-start(bf16[72,48]{1,0:T(8,128)(2,1)} %constant.20.clone.right_ref) | copy-start | bytes 20740
  12.6 19.8 %copy-start.13 = (bf16[72,48]{1,0:T(8,128)(2,1)S(1)}, bf16[72,48]{1,0:T(8,128)(2,1)}, u32[]{:S(2)}) copy-start(bf16[72,48]{1,0:T(8,128)(2,1)} %constant.19.clone.left_ref) | copy-start | bytes 20740
  12.6 19.7 %collective-permute-start.5 = (bf16[2,12,3,8,128]{4,3,2,1,0:T(8,128)(2,1)S(1)}, bf16[2,12,3,8,128]{4,3,2,1,0:T(8,128)(2,1)S(1)}, u32[]{:S(2)}, u32[]{:S(2)}) collective-permute-start(bf16[2,12,3,8,128]{4,3,2,1,0:T(8,128)(2,1)S(1)} %get-tuple-element.16), channel_id=1, source_target_pairs={{8,0},{9,1},{10,2},{11,3},{12,4},{13,5},{14,6},{15,7},{16,8},{17,9... | collective-permute-start | bytes 442376 | tf_op jit(solution)/shard_map/ppermute | solution.py:379

commit v4 on v3

--- a/solution.py
+++ b/solution.py
@@ -246,6 +246,7 @@
         return jnp.concatenate([v, v[:, : C - 128]], axis=1)
 
     halves = [(latw, c) for latw in range(2) for c in range(UNITS)]
+    groups = [(latw, [c for c in (2 * m - 1, 2 * m) if 0 <= c < UNITS]) for latw in range(2) for m in range(WINS)]
 
     def gather(z, latw):
         levels = pl.ds(2 * z, 2)
@@ -292,16 +293,19 @@
         e = jnp.exp2(s - jnp.max(s, axis=0, keepdims=True))
         return (e * (1.0 / jnp.sum(e, axis=0, keepdims=True))).astype(BF16)
 
-    def attend(latw, c, p):
-        m, half = unit_place(c)
+    def attend(latw, units, p):
+        m, half = unit_place(units[0])
         r0 = ROWS * latw + 144 * m
-        o = tn(p, kvs[r0 : r0 + 144, C:])
-        out = o[0:SLOT]
-        for h in range(1, HEADS):
-            out = jnp.where(lane == h, o[head_row(h) : head_row(h) + SLOT], out)
-        to = SLOT * (UNITS * latw + c)
-        os_[to : to + SLOT] = out
-        rs[to : to + SLOT] = xs[r0 + 32 * half : r0 + 32 * half + SLOT]
+        both_halves = tn(p, kvs[r0 : r0 + 144, C:])
+        for k, c in enumerate(units):
+            o = both_halves[256 * k : 256 * k + 256]
+            out = o[0:SLOT]
+            for h in range(1, HEADS):
+                out = jnp.where(lane == h, o[head_row(h) : head_row(h) + SLOT], out)
+            m, half = unit_place(c)
+            to = SLOT * (UNITS * latw + c)
+            os_[to : to + SLOT] = out
+            rs[to : to + SLOT] = xs[r0 + 32 * half : r0 + 32 * half + SLOT]
 
     def level_pair(z):
         for latw in range(2):
@@ -315,13 +319,14 @@
             ss[n] = scores(z, latw, c)
         for n in range(2 * UNITS):
             ps[n] = soft(ss[n])
-        for n, (latw, c) in enumerate(halves):
-            attend(latw, c, ps[n])
+        for latw, units in groups:
+            k = UNITS * latw + units[0]
+            attend(latw, units, ps[k] if len(units) == 1 else jnp.concatenate([ps[k], ps[k + 1]], axis=1))
         resid = rs[...] + nn(os_[...].astype(BF16), wproj_ref[...])
         mean = jnp.mean(resid, axis=1, keepdims=True)
         cen = resid - mean
-        var = nn((cen * cen).astype(BF16), ones) * (1.0 / C)
-        normed = (cen * both(lax.rsqrt(var + EPS)) * gm_ref[...]).astype(BF16)
+        var = jnp.mean(cen * cen, axis=1, keepdims=True)
+        normed = (cen * lax.rsqrt(var + EPS) * gm_ref[...]).astype(BF16)
         u = nn(normed, wup_ref[...])
         w = u * u
         poly = w * GELU[-1] + GELU[-2]

time: 61.7 us -> 60.8 us (0.985)
  Pallas kernels: 40.6 us -> 39.6 us
    pallas_call x1, Pallas kernels: 28.7 us -> 27.7 us  [run_block(): pl.pallas_call(block_kernel, out_shape=jax.ShapeDtypeStruct(tokens.shape,...]
  transfers between devices with their start and end apart: 7 -> 7, of which waited for: 1 -> 1; matrix products, arithmetic and copies ran while one was open for 0% -> 0% of each run, Pallas kernels for 19% -> 20%
where the time goes in v4:
time: 60.8 us; the launch traced here: 60.3 us
  Pallas kernels  39.6 us (65%)
  starting transfers between devices  15.4 us (25%)
  waiting for transfers between devices  3.24 us (5%)
  local copies, waits for them, and re-layouts  1.56 us (3%)
    pallas_call x1, Pallas kernels, run_block(): pl.pallas_call(block_kernel, out_shape=jax.ShapeDtypeStruct(tokens.shape,...  27.7 us
    ppermute x7, starting transfers between devices, passed_along(): return lax.ppermute(block, ('lat', 'lon'), route)  15.4 us
    pallas_call x1, Pallas kernels, make_bias(): pl.pallas_call(bias_kernel, out_shape=jax.ShapeDtypeStruct((2, ZW, 2, 144...  10.9 us
    ppermute x7, waiting for transfers between devices, passed_along(): return lax.ppermute(block, ('lat', 'lon'), route)  3.24 us
    unnamed x28, local copies, waits for them, and re-layouts  1.56 us
  transfers between devices with their start and end apart: 7, of which 1 were waited for; matrix products, arithmetic and copies ran while one was open for 0% of the time, Pallas kernels for 20%

profile of v4, /device:TPU:0, one launch (start us, length us, event | category | flops | bytes accessed | tf_op | source)
XLA Modules:
  0.0 60.3 jit_solution(7723568435063289215)
XLA Ops:
  0.0 0.0 collective-permute-start.6
  0.0 0.0 copy-start
  0.0 1.5 %copy-done = bf16[8,6,72,192]{3,2,1,0:T(8,128)(2,1)S(1)} copy-done((bf16[8,6,72,192]{3,2,1,0:T(8,128)(2,1)S(1)}, bf16[8,6,72,192]{3,2,1,0:T(8,128)(2,1)}, u32[]{:S(2)}) %copy-start) | copy-done | bytes 1327128
  1.5 0.0 copy-start.2
  1.5 0.0 copy-start.6
  1.5 1.0 %shard_map.127 = (bf16[12,3,72,128]{3,2,1,0:T(8,128)(2,1)S(1)}, bf16[12,3,72,128]{3,2,1,0:T(8,128)(2,1)S(1)}, bf16[12,6,8,128]{3,2,1,0:T(8,128)(2,1)}, bf16[12,6,8,128]{3,2,1,0:T(8,128)(2,1)}) custom-call(bf16[8,6,72,192]{3,2,1,0:T(8,128)(2,1)S(1)} %copy-done), custom_call_target="tpu_custom_call" | custom-call | tf_op jit(solution)/shard_map/pallas_call | solution.py:211
  2.5 1.6 %collective-permute-start.2 = (bf16[12,6,8,128]{3,2,1,0:T(8,128)(2,1)}, bf16[12,6,8,128]{3,2,1,0:T(8,128)(2,1)S(1)}, u32[]{:S(2)}, u32[]{:S(2)}) collective-permute-start(bf16[12,6,8,128]{3,2,1,0:T(8,128)(2,1)} %get-tuple-element.13), channel_id=1, source_target_pairs={{7,0},{0,1},{1,2},{2,3},{3,4},{4,5},{5,6},{6,7},{15,8},{8,9},{9,10... | collective-permute-start | bytes 442376 | tf_op jit(solution)/shard_map/ppermute | solution.py:384
  4.1 2.6 %collective-permute-start.3 = (bf16[12,6,8,128]{3,2,1,0:T(8,128)(2,1)}, bf16[12,6,8,128]{3,2,1,0:T(8,128)(2,1)S(1)}, u32[]{:S(2)}, u32[]{:S(2)}) collective-permute-start(bf16[12,6,8,128]{3,2,1,0:T(8,128)(2,1)} %get-tuple-element.14), channel_id=1, source_target_pairs={{1,0},{2,1},{3,2},{4,3},{5,4},{6,5},{7,6},{0,7},{9,8},{10,9},{11,1... | collective-permute-start | bytes 442376 | tf_op jit(solution)/shard_map/ppermute | solution.py:384
  6.7 2.8 %collective-permute-start = (bf16[12,3,72,128]{3,2,1,0:T(8,128)(2,1)S(1)}, bf16[12,3,72,128]{3,2,1,0:T(8,128)(2,1)S(1)}, u32[]{:S(2)}, u32[]{:S(2)}) collective-permute-start(bf16[12,3,72,128]{3,2,1,0:T(8,128)(2,1)S(1)} %get-tuple-element.11), channel_id=1, source_target_pairs={{120,0},{121,1},{122,2},{123,3},{124,4},{125,5},{126,6},{127,7},{0... | collective-permute-start | bytes 1990664 | tf_op jit(solution)/shard_map/ppermute | solution.py:384
  9.5 2.8 %collective-permute-start.1 = (bf16[12,3,72,128]{3,2,1,0:T(8,128)(2,1)S(1)}, bf16[12,3,72,128]{3,2,1,0:T(8,128)(2,1)S(1)}, u32[]{:S(2)}, u32[]{:S(2)}) collective-permute-start(bf16[12,3,72,128]{3,2,1,0:T(8,128)(2,1)S(1)} %get-tuple-element.12), channel_id=1, source_target_pairs={{8,0},{9,1},{10,2},{11,3},{12,4},{13,5},{14,6},{15,7},{16,8},{17,9... | collective-permute-start | bytes 1990664 | tf_op jit(solution)/shard_map/ppermute | solution.py:384
  12.3 0.1 add_convert_fusion.cut_ref
  12.4 0.0 collective-permute-done.2.l_ref
  12.4 0.0 collective-permute-done.3.r_ref
  12.4 0.1 collective-permute-start.4
  12.5 0.0 copy-start.1
  12.5 0.0 copy-start.3
  12.5 0.0 copy-start.4
  12.5 0.0 copy-start.5
  12.5 0.0 copy-start.7
  12.5 0.0 copy-start.8
  12.6 0.0 copy-start.9
  12.6 0.0 copy-start.10
  12.6 0.0 copy-start.11
  12.6 0.0 copy-start.12
  12.6 0.0 copy-start.13
  12.6 5.6 %collective-permute-start.5 = (bf16[2,12,3,8,128]{4,3,2,1,0:T(8,128)(2,1)S(1)}, bf16[2,12,3,8,128]{4,3,2,1,0:T(8,128)(2,1)S(1)}, u32[]{:S(2)}, u32[]{:S(2)}) collective-permute-start(bf16[2,12,3,8,128]{4,3,2,1,0:T(8,128)(2,1)S(1)} %get-tuple-element.16), channel_id=1, source_target_pairs={{8,0},{9,1},{10,2},{11,3},{12,4},{13,5},{14,6},{15,7},{16,8},{17,9... | collective-permute-start | bytes 442376 | tf_op jit(solution)/shard_map/ppermute | solution.py:384
  18.2 0.0 collective-permute-done.6.table0_ref
  18.2 0.0 copy-done.2
  18.2 0.0 copy-done.6
  18.2 10.9 %shard_map.129.bias_ref = f32[2,4,2,144,256]{4,3,2,1,0:T(8,128)S(1)} custom-call(s32[2]{0:T(128)S(1)} %add_convert_fusion.cut_ref, f32[1,6,4,3312]{3,2,1,0:T(4,128)S(1)} %bitcast.7, f32[1,6,4,3312]{3,2,1,0:T(4,128)} %collective-permute-done.6.table0_ref, s32[144,144]{1,0:T(8,128)S(1)} %copy-done.6), custom_call_target="tpu_custom_call" | custom-call | flops 14000000000 | bytes 2000000 | tf_op jit(solution)/shard_map/pallas_call | solution.py:164
  29.1 3.2 %collective-permute-done.4.cp_ref = bf16[2,12,3,8,128]{4,3,2,1,0:T(8,128)(2,1)S(1)} collective-permute-done((bf16[2,12,3,8,128]{4,3,2,1,0:T(8,128)(2,1)S(1)}, bf16[2,12,3,8,128]{4,3,2,1,0:T(8,128)(2,1)S(1)}, u32[]{:S(2)}, u32[]{:S(2)}) %collective-permute-start.4) | collective-permute-done | bytes 147488 | tf_op jit(solution)/shard_map/ppermute | solution.py:384
  32.3 0.0 collective-permute-done.5.cn_ref
  32.3 0.0 collective-permute-done.prev_ref
  32.3 0.0 collective-permute-done.1.next_ref
  32.3 0.0 copy-done.1
  32.3 0.0 copy-done.3
  32.3 0.0 copy-done.4
  32.3 0.0 copy-done.5
  32.3 0.0 copy-done.7
  32.3 0.0 copy-done.8
  32.4 0.0 copy-done.9
  32.4 0.0 copy-done.10
  32.4 0.0 copy-done.11
  32.4 0.0 copy-done.12
  32.4 0.0 copy-done.13
  32.4 27.7 %shard_map.130 = bf16[8,6,72,192]{3,2,1,0:T(8,128)(2,1)} custom-call(bf16[8,6,72,192]{3,2,1,0:T(8,128)(2,1)S(1)} %copy-done.1, bf16[12,3,72,128]{3,2,1,0:T(8,128)(2,1)S(1)} %collective-permute-done.prev_ref, bf16[12,3,72,128]{3,2,1,0:T(8,128)(2,1)S(1)} %collective-permute-done.1.next_ref, bf16[12,6,8,128]{3,2,1,0:T(8,128)(2,1)S(1)} %collective-permute-done.2.l_ref, ...), custom_call_target="tpu_custom_call" | custom-call | flops 30000001024 | bytes 2000000 | tf_op jit(solution)/shard_map/pallas_call | solution.py:357
  (1 shorter events, 0.0 us)
Async XLA Ops:
  0.0 18.2 %collective-permute-start.6 = (f32[1,6,4,3312]{3,2,1,0:T(4,128)}, f32[1,6,4,3312]{3,2,1,0:T(4,128)}, u32[]{:S(2)}, u32[]{:S(2)}) collective-permute-start(f32[1,6,4,3312]{3,2,1,0:T(4,128)} %bitcast.6), channel_id=1, source_target_pairs={{120,0},{121,1},{122,2},{123,3},{124,4},{125,5},{126,6},{127,7},{0... | collective-permute-start | bytes 953864 | tf_op jit(solution)/shard_map/ppermute | solution.py:384
  0.0 1.5 %copy-start = (bf16[8,6,72,192]{3,2,1,0:T(8,128)(2,1)S(1)}, bf16[8,6,72,192]{3,2,1,0:T(8,128)(2,1)}, u32[]{:S(2)}) copy-start(bf16[8,6,72,192]{3,2,1,0:T(8,128)(2,1)} %own_ref.1) | copy-start | bytes 3981316
  1.5 16.7 %copy-start.2 = (f32[1,4,6,3312]{3,1,2,0:T(4,128)S(1)}, f32[1,4,6,3312]{3,1,2,0:T(4,128)}, u32[]{:S(2)}) copy-start(f32[1,4,6,3312]{3,1,2,0:T(4,128)} %param.14) | copy-start | bytes 953860
  1.5 16.7 %copy-start.6 = (s32[144,144]{1,0:T(8,128)S(1)}, s32[144,144]{1,0:T(8,128)}, u32[]{:S(2)}) copy-start(s32[144,144]{1,0:T(8,128)} %index_ref.1) | copy-start | bytes 248836
  2.5 9.8 %collective-permute-start.2 = (bf16[12,6,8,128]{3,2,1,0:T(8,128)(2,1)}, bf16[12,6,8,128]{3,2,1,0:T(8,128)(2,1)S(1)}, u32[]{:S(2)}, u32[]{:S(2)}) collective-permute-start(bf16[12,6,8,128]{3,2,1,0:T(8,128)(2,1)} %get-tuple-element.13), channel_id=1, source_target_pairs={{7,0},{0,1},{1,2},{2,3},{3,4},{4,5},{5,6},{6,7},{15,8},{8,9},{9,10... | collective-permute-start | bytes 442376 | tf_op jit(solution)/shard_map/ppermute | solution.py:384
  4.1 8.3 %collective-permute-start.3 = (bf16[12,6,8,128]{3,2,1,0:T(8,128)(2,1)}, bf16[12,6,8,128]{3,2,1,0:T(8,128)(2,1)S(1)}, u32[]{:S(2)}, u32[]{:S(2)}) collective-permute-start(bf16[12,6,8,128]{3,2,1,0:T(8,128)(2,1)} %get-tuple-element.14), channel_id=1, source_target_pairs={{1,0},{2,1},{3,2},{4,3},{5,4},{6,5},{7,6},{0,7},{9,8},{10,9},{11,1... | collective-permute-start | bytes 442376 | tf_op jit(solution)/shard_map/ppermute | solution.py:384
  6.7 25.6 %collective-permute-start = (bf16[12,3,72,128]{3,2,1,0:T(8,128)(2,1)S(1)}, bf16[12,3,72,128]{3,2,1,0:T(8,128)(2,1)S(1)}, u32[]{:S(2)}, u32[]{:S(2)}) collective-permute-start(bf16[12,3,72,128]{3,2,1,0:T(8,128)(2,1)S(1)} %get-tuple-element.11), channel_id=1, source_target_pairs={{120,0},{121,1},{122,2},{123,3},{124,4},{125,5},{126,6},{127,7},{0... | collective-permute-start | bytes 1990664 | tf_op jit(solution)/shard_map/ppermute | solution.py:384
  9.5 22.8 %collective-permute-start.1 = (bf16[12,3,72,128]{3,2,1,0:T(8,128)(2,1)S(1)}, bf16[12,3,72,128]{3,2,1,0:T(8,128)(2,1)S(1)}, u32[]{:S(2)}, u32[]{:S(2)}) collective-permute-start(bf16[12,3,72,128]{3,2,1,0:T(8,128)(2,1)S(1)} %get-tuple-element.12), channel_id=1, source_target_pairs={{8,0},{9,1},{10,2},{11,3},{12,4},{13,5},{14,6},{15,7},{16,8},{17,9... | collective-permute-start | bytes 1990664 | tf_op jit(solution)/shard_map/ppermute | solution.py:384
  12.4 19.9 %collective-permute-start.4 = (bf16[2,12,3,8,128]{4,3,2,1,0:T(8,128)(2,1)S(1)}, bf16[2,12,3,8,128]{4,3,2,1,0:T(8,128)(2,1)S(1)}, u32[]{:S(2)}, u32[]{:S(2)}) collective-permute-start(bf16[2,12,3,8,128]{4,3,2,1,0:T(8,128)(2,1)S(1)} %get-tuple-element.15), channel_id=1, source_target_pairs={{120,0},{121,1},{122,2},{123,3},{124,4},{125,5},{126,6},{127,7},{0... | collective-permute-start | bytes 442376 | tf_op jit(solution)/shard_map/ppermute | solution.py:384
  12.5 19.8 %copy-start.1 = (bf16[8,6,72,192]{3,2,1,0:T(8,128)(2,1)S(1)}, bf16[8,6,72,192]{3,2,1,0:T(8,128)(2,1)}, u32[]{:S(2)}) copy-start(bf16[8,6,72,192]{3,2,1,0:T(8,128)(2,1)} %own_ref.1) | copy-start | bytes 3981316
  12.5 19.8 %copy-start.3 = (bf16[192,768]{1,0:T(8,128)(2,1)S(1)}, bf16[192,768]{1,0:T(8,128)(2,1)}, u32[]{:S(2)}) copy-start(bf16[192,768]{1,0:T(8,128)(2,1)} %wup_ref.1) | copy-start | bytes 884740
  12.5 19.8 %copy-start.4 = (bf16[768,192]{0,1:T(8,128)(2,1)S(1)}, bf16[768,192]{0,1:T(8,128)(2,1)}, u32[]{:S(2)}) copy-start(bf16[768,192]{0,1:T(8,128)(2,1)} %param.21) | copy-start | bytes 884740
  12.5 19.8 %copy-start.5 = (bf16[192,576]{1,0:T(8,128)(2,1)S(1)}, bf16[192,576]{1,0:T(8,128)(2,1)}, u32[]{:S(2)}) copy-start(bf16[192,576]{1,0:T(8,128)(2,1)} %wqkv_ref.1) | copy-start | bytes 663556
  12.5 19.8 %copy-start.7 = (bf16[192,192]{1,0:T(8,128)(2,1)S(1)}, bf16[192,192]{1,0:T(8,128)(2,1)}, u32[]{:S(2)}) copy-start(bf16[192,192]{1,0:T(8,128)(2,1)} %wproj_ref.1) | copy-start | bytes 221188
  12.5 19.8 %copy-start.8 = (f32[192]{0:T(256)S(1)}, f32[192]{0:T(256)}, u32[]{:S(2)}) copy-start(f32[192]{0:T(256)} %param.16) | copy-start | bytes 2308
  12.6 19.8 %copy-start.9 = (f32[192]{0:T(256)S(1)}, f32[192]{0:T(256)}, u32[]{:S(2)}) copy-start(f32[192]{0:T(256)} %param.19) | copy-start | bytes 2308
  12.6 19.8 %copy-start.10 = (bf16[504,432]{1,0:T(8,128)(2,1)S(1)}, bf16[504,432]{1,0:T(8,128)(2,1)}, u32[]{:S(2)}) copy-start(bf16[504,432]{1,0:T(8,128)(2,1)} %constant.18.clone.perm_ref) | copy-start | bytes 1306372
  12.6 19.8 %copy-start.11 = (bf16[440,480]{1,0:T(8,128)(2,1)S(1)}, bf16[440,480]{1,0:T(8,128)(2,1)}, u32[]{:S(2)}) copy-start(bf16[440,480]{1,0:T(8,128)(2,1)} %constant.21.clone.back_ref) | copy-start | bytes 1267204
  12.6 19.8 %copy-start.12 = (bf16[72,48]{1,0:T(8,128)(2,1)S(1)}, bf16[72,48]{1,0:T(8,128)(2,1)}, u32[]{:S(2)}) copy-start(bf16[72,48]{1,0:T(8,128)(2,1)} %constant.20.clone.right_ref) | copy-start | bytes 20740
  12.6 19.8 %copy-start.13 = (bf16[72,48]{1,0:T(8,128)(2,1)S(1)}, bf16[72,48]{1,0:T(8,128)(2,1)}, u32[]{:S(2)}) copy-start(bf16[72,48]{1,0:T(8,128)(2,1)} %constant.19.clone.left_ref) | copy-start | bytes 20740
  12.6 19.7 %collective-permute-start.5 = (bf16[2,12,3,8,128]{4,3,2,1,0:T(8,128)(2,1)S(1)}, bf16[2,12,3,8,128]{4,3,2,1,0:T(8,128)(2,1)S(1)}, u32[]{:S(2)}, u32[]{:S(2)}) collective-permute-start(bf16[2,12,3,8,128]{4,3,2,1,0:T(8,128)(2,1)S(1)} %get-tuple-element.16), channel_id=1, source_target_pairs={{8,0},{9,1},{10,2},{11,3},{12,4},{13,5},{14,6},{15,7},{16,8},{17,9... | collective-permute-start | bytes 442376 | tf_op jit(solution)/shard_map/ppermute | solution.py:384
